TPU v7x, 32 devices: a whole 2x2x4 slice. The times are simulated.
32 devices in a mesh: dp: 8 (over z, y), nbr: 4 (over x, core).
Axes of the slice: x: 2, y: 2, z: 4, core: 2. Of those that a mesh axis runs over, the one named last changes fastest.
Arguments:
- queries: bfloat16 [6144, 4096], P(('dp', 'nbr')), may hold values from -256 to 256
- cotangent: bfloat16 [6144, 4096], P(('dp', 'nbr')), may hold values from -1 to 1
- pool: bfloat16 [64, 128, 896], P('dp', 'nbr'), may hold values from -60 to 60
- enc_gain: float32 [896], replicated, may hold values from 0.25 to 1.75
- enc_weight: bfloat16 [896, 896], replicated, may hold values from -0.1875 to 0.1875
- k_weight: bfloat16 [896, 4096], P(None, 'nbr'), may hold values from -0.1875 to 0.1875
- v_weight: bfloat16 [896, 4096], P(None, 'nbr'), may hold values from -0.1875 to 0.1875
- nbr_owner: int32 [96, 1], replicated, may hold values from 0 to 7; in each aligned block of 12 rows (0 to 11, 12 to 23, ...) at most 2 rows name the same one
- nbr_slot: int32 [96, 1], replicated, may hold values from 0 to 7
Outputs:
- attended: bfloat16 [6144, 4096], P(('dp', 'nbr'))
- grad_k: float32 [896, 4096], P('dp', 'nbr')
- grad_v: float32 [896, 4096], P('dp', 'nbr')
Inputs may be any that keep to these rules, and one draw needn't show every extreme that they name: `nbr_owner`: within the 12 groups of one sequence at most 2 name the same index of dp, and this bound is reached.
All inputs are finite; a program needn't handle non-finite values.
Results may differ from a plain program's by a relative error of at most 0.035.
The roundings to bfloat16 on the way count: a program that leaves them out, or rounds other values in their place, can miss the bound.
Values may be sent and summed in bfloat16 or wider, within the bound.
A program may use at most 128 MiB of HBM per device.

v0:
```python
import jax
import jax.numpy as jnp
from jax import lax
from jax.sharding import PartitionSpec as P

HEAD = 128
GROUP = 64
NB = 8


def encode(blocks, gain_vec, weight):
    widened = blocks.astype(jnp.float32)
    mean_sq = jnp.mean(widened * widened, axis=-1, keepdims=True)
    normed = (widened * lax.rsqrt(mean_sq + 1e-06) * gain_vec).astype(jnp.bfloat16)
    feature_width = blocks.shape[-1]
    combined = jnp.dot(
        normed.reshape(-1, feature_width), weight, preferred_element_type=jnp.float32
    )
    return (widened + jax.nn.gelu(combined.reshape(widened.shape))).astype(jnp.bfloat16)


def attend(q_heads, key_rows, value_rows, group_len):
    offset_rows = group_len - 1
    seq_len, head_count, head_size = q_heads.shape
    blank_rows = jnp.zeros((offset_rows, head_count, head_size), q_heads.dtype)
    shifted = jnp.concatenate([q_heads[offset_rows:], blank_rows], axis=0)
    shifted = shifted.reshape(-1, group_len, head_count, head_size)
    scores = jnp.einsum("cqhd,ckhd->chqk", shifted, key_rows, preferred_element_type=jnp.float32)
    scores = scores * head_size ** (-0.5)
    weights = jax.nn.softmax(scores, axis=-1).astype(jnp.bfloat16)
    combined = jnp.einsum(
        "chqk,ckhd->cqhd", weights, value_rows, preferred_element_type=jnp.float32
    )
    combined = combined.astype(jnp.bfloat16).reshape(seq_len, head_count, head_size)
    return jnp.concatenate([blank_rows, combined[: seq_len - offset_rows]], axis=0)


def per_device(
    queries, cotangent, pool, enc_gain, enc_weight, k_weight, v_weight, nbr_owner, nbr_slot
):
    dp_count = lax.axis_size("dp")
    my_lane = lax.axis_index("dp")
    q_rows, g_rows = (
        lax.all_to_all(queries, "nbr", split_axis=1, concat_axis=0, tiled=True),
        lax.all_to_all(cotangent, "nbr", split_axis=1, concat_axis=0, tiled=True),
    )
    seq_len = q_rows.shape[0]
    heads_here = q_rows.shape[1] // HEAD
    per_row = seq_len // GROUP
    owned_enc = encode(pool, enc_gain, enc_weight)
    owners = nbr_owner[:, 0].reshape(dp_count, per_row)
    slot_ids = nbr_slot[:, 0].reshape(dp_count, per_row)
    my_owner = lax.dynamic_slice_in_dim(owners, my_lane, 1, 0)[0]
    my_slot = lax.dynamic_slice_in_dim(slot_ids, my_lane, 1, 0)[0]
    pooled = lax.all_gather(owned_enc, "dp", axis=0, tiled=True)
    picked = jnp.take(pooled, my_owner * NB + my_slot, axis=0)
    neighbours = lax.all_gather(picked, "nbr", axis=1, tiled=True)
    enc_width = neighbours.shape[2]
    block_len = neighbours.shape[1]
    flat_enc = neighbours.reshape(-1, enc_width)
    key_rows = jnp.dot(flat_enc, k_weight, preferred_element_type=jnp.float32).astype(jnp.bfloat16)
    value_rows = jnp.dot(flat_enc, v_weight, preferred_element_type=jnp.float32).astype(
        jnp.bfloat16
    )
    q_heads = q_rows.reshape(seq_len, heads_here, HEAD)

    def attend_here(keys_in, values_in):
        shaped_keys = keys_in.reshape(per_row, block_len, heads_here, HEAD)
        shaped_values = values_in.reshape(per_row, block_len, heads_here, HEAD)
        return attend(q_heads, shaped_keys, shaped_values, GROUP).reshape(seq_len, -1)

    attended, pullback = jax.vjp(attend_here, key_rows, value_rows)
    key_grads, value_grads = pullback(g_rows)
    merged = lax.all_to_all(attended, "nbr", split_axis=0, concat_axis=1, tiled=True)
    contract = (((0,), (0,)), ((), ()))
    grad_key = lax.dot_general(flat_enc, key_grads, contract, preferred_element_type=jnp.float32)
    grad_value = lax.dot_general(
        flat_enc, value_grads, contract, preferred_element_type=jnp.float32
    )
    summed = lax.psum_scatter(
        jnp.concatenate([grad_key, grad_value], axis=1), "dp", scatter_dimension=0, tiled=True
    )
    split_at = key_grads.shape[1]
    return (merged, summed[:, :split_at], summed[:, split_at:])


def solution(mesh):
    return jax.shard_map(
        per_device,
        mesh=mesh,
        in_specs=(
            P(("dp", "nbr"), None),
            P(("dp", "nbr"), None),
            P("dp", "nbr", None),
            P(),
            P(),
            P(None, "nbr"),
            P(None, "nbr"),
            P(),
            P(),
        ),
        out_specs=(P(("dp", "nbr"), None), P("dp", "nbr"), P("dp", "nbr")),
        check_vma=False,
    )
```

profile of v0, /device:TPU:0, one launch (start us, length us, event | category | flops | bytes accessed | tf_op | source)
XLA Modules:
  0.0 372.3 jit_solution(8618419077092401863)
XLA Ops:
  7.2 1.3 fusion.48
  8.6 3.3 fusion.51
  11.9 0.5 broadcast.110
  12.4 0.7 reduce.7
  13.1 0.7 reduce.6
  13.8 0.1 reshape_squeeze.7
  14.0 67.5 %all-gather.3.cloned.1.call-done = bf16[64,32,896]{2,1,0:T(8,128)(2,1)} async-done(((bf16[8,32,896]{2,1,0:T(8,128)(2,1)}), bf16[64,32,896]{2,1,0:T(8,128)(2,1)}) %all-gather.3.cloned.1.call-update) | async-done | bytes 3670032 | tf_op jit(solution)/shard_map/all_gather | solution.py:55
  81.5 2.7 gather_fusion
  84.2 1.0 broadcast_select_fusion
  85.2 2.7 copy.98
  87.9 3.6 all-to-all-start
  91.5 3.0 copy.97
  94.5 30.9 %all-to-all-done = bf16[192,4,1024]{2,0,1:T(8,128)(2,1)S(1)} async-done(((bf16[192,4,1024]{2,0,1:T(8,128)(2,1)}), bf16[192,4,1024]{2,0,1:T(8,128)(2,1)S(1)}, u32[]{:S(2)}, u32[]{:S(2)}) %all-to-all-start) | async-done | bytes 1572896 | tf_op jit(solution)/shard_map/all_to_all | solution.py:44
  125.4 4.3 %all-to-all-start.2 = ((bf16[192,4,1024]{2,0,1:T(8,128)(2,1)}), bf16[192,4,1024]{2,0,1:T(8,128)(2,1)}, u32[]{:S(2)}, u32[]{:S(2)}) async-start(bf16[192,4,1024]{2,0,1:T(8,128)(2,1)} %bitcast.81), calls=%async_computation.2 | async-start | bytes 3145728 | tf_op jit(solution)/shard_map/all_to_all | solution.py:45
  129.8 0.4 copy.53
  130.3 0.1 slice.18
  130.4 19.5 %all-to-all-done.2 = bf16[192,4,1024]{2,0,1:T(8,128)(2,1)} async-done(((bf16[192,4,1024]{2,0,1:T(8,128)(2,1)}), bf16[192,4,1024]{2,0,1:T(8,128)(2,1)}, u32[]{:S(2)}, u32[]{:S(2)}) %all-to-all-start.2) | async-done | bytes 1572896 | tf_op jit(solution)/shard_map/all_to_all | solution.py:45
  149.9 1.8 copy.56
  151.8 0.1 split.4
  151.9 1.3 concatenate.9
  153.1 1.3 pad.5
  154.4 5.4 %fusion.26 = bf16[192,8,8,128]{3,1,2,0:T(8,128)(2,1)S(1)} fusion(bf16[1536,896]{1,0:T(8,128)(2,1)} %bitcast.94, bf16[896,1024]{1,0:T(8,128)(2,1)S(1)} %copy-done), kind=kOutput, calls=%fused_computation.32 | convolution fusion | flops 2820145152 | bytes 7733248 | tf_op jit(solution)/shard_map/dot_general | solution.py:61
  159.8 0.8 copy.54
  160.7 0.9 copy-done.5
  161.6 0.6 copy-done.7
  162.2 3.6 fusion.25
  165.8 0.8 copy.55
  166.6 0.5 copy-done.3
  167.2 2.3 fusion.14
  169.4 1.7 copy-done.2
  171.2 2.6 fusion.84
  173.8 16.8 %convert_bitcast_fusion = bf16[12,128,8,128]{1,3,2,0:T(8,128)(2,1)} fusion(bf16[12,64,8,128]{3,2,1,0:T(8,128)(2,1)} %bitcast.78, f32[12,8,64]{2,1,0:T(8,128)S(1)} %get-tuple-element.7, f32[12,8,64,128]{3,2,1,0:T(8,128)} %copy-done.2), kind=kOutput, calls=%fused_computation.21 | convolution fusion | flops 206837888 | bytes 7888896 | tf_op jit(solution)/shard_map/transpose(jvp(chqk,ckhd->cqhd))/dot_general | solution.py:31
  190.6 5.3 %fusion.7 = (f32[12,8,64]{2,1,0:T(8,128)S(1)}, bf16[12,8,64,128]{3,2,1,0:T(8,128)(2,1)}) fusion(f32[12,8,64,128]{3,2,1,0:T(8,128)} %get-tuple-element.8, f32[12,8,64]{2,1,0:T(8,128)S(1)} %multiply_divide_fusion, bf16[12,128,8,128]{3,2,1,0:T(8,128)(2,1)S(1)} %bitcast.75, bf16[12,64,8,128]{3,2,1,0:T(8,128)(2,1)} %bitcast.79), kind=kOutput, calls=%fused_computation.12 | convolution fusion | flops 205252608 | bytes 9486336 | tf_op jit(solution)/shard_map/transpose(jvp(chqk,ckhd->cqhd))/dot_general | solution.py:31
  195.9 4.8 %copy.49 = bf16[12,128,8,128]{3,2,1,0:T(8,128)(2,1)} copy(bf16[12,128,8,128]{1,3,2,0:T(8,128)(2,1)} %convert_bitcast_fusion) | data formatting | bytes 6291456 | tf_op jit(solution)/shard_map/transpose(jvp(chqk,ckhd->cqhd))/convert_element_type | solution.py:31
  200.7 17.4 %convert_bitcast_fusion.1 = bf16[12,128,8,128]{3,1,2,0:T(8,128)(2,1)} fusion(bf16[12,8,64,128]{3,2,1,0:T(8,128)(2,1)} %get-tuple-element.10, f32[12,8,64]{2,1,0:T(8,128)S(1)} %neg.6, f32[12,8,64]{2,1,0:T(8,128)S(1)} %get-tuple-element.7, bf16[12,64,8,128]{3,2,1,0:T(8,128)(2,1)} %bitcast.84, f32[12,8,64,128]{3,2,1,0:T(8,128)} %copy-done.2), kind=kOutput, calls=%fused_computation.22 | convolution fusion | flops 209197184 | bytes 9486336 | tf_op jit(solution)/shard_map/transpose(jvp(cqhd,ckhd->chqk))/dot_general | solution.py:28
  218.1 4.5 %copy.48 = bf16[12,128,8,128]{3,2,1,0:T(8,128)(2,1)S(1)} copy(bf16[12,128,8,128]{3,1,2,0:T(8,128)(2,1)} %convert_bitcast_fusion.1) | data formatting | bytes 6291456 | tf_op jit(solution)/shard_map/transpose(jvp(cqhd,ckhd->chqk))/convert_element_type | solution.py:28
  222.6 3.1 fusion.11
  225.7 3.1 fusion.8
  228.8 3.5 pad_maximum_fusion
  232.3 14.6 %fusion.41 = bf16[12,64,8,128]{3,1,2,0:T(8,128)(2,1)} fusion(bf16[12,128,8,128]{3,2,1,0:T(8,128)(2,1)S(1)} %bitcast.76, f32[12,8,64]{2,1,0:T(8,128)S(1)} %get-tuple-element.7, f32[12,8,64,128]{3,2,1,0:T(8,128)} %copy-done.2), kind=kOutput, calls=%fused_computation.45 | convolution fusion | flops 206051456 | bytes 7888896 | tf_op jit(solution)/shard_map/jvp(chqk,ckhd->cqhd)/dot_general | solution.py:31
  246.9 2.7 copy.42
  249.6 0.1 slice.19
  249.7 0.1 concatenate.10
  249.8 0.7 all_to_all.41
  250.6 22.7 %all_to_all.51 = bf16[4,192,1024]{2,1,0:T(8,128)(2,1)S(1)} all-to-all(bf16[4,192,1024]{2,1,0:T(8,128)(2,1)S(1)} %all_to_all.41), channel_id=1, replica_groups=mesh['dp'=8,'nbr'=4] {'nbr'}, dimensions={0} | all-to-all | bytes 3145728 | tf_op jit(solution)/shard_map/all_to_all | solution.py:74
  273.2 1.3 copy.52
  274.5 89.0 %reduce-scatter.2.cloned.1.call-done = f32[112,2048]{1,0:T(8,128)} async-done(((f32[896,2048]{1,0:T(8,128)}), f32[112,2048]{1,0:T(8,128)}) %reduce-scatter.2.cloned.1.call-update) | async-done | bytes 917520 | tf_op jit(solution)/shard_map/reduce_scatter | solution.py:80
  363.6 2.2 fusion.83
  (30 shorter events, 0.3 us)
Async XLA Ops:
  7.2 147.2 %copy-start = (bf16[896,1024]{1,0:T(8,128)(2,1)S(1)}, bf16[896,1024]{1,0:T(8,128)(2,1)}, u32[]{:S(2)}) copy-start(bf16[896,1024]{1,0:T(8,128)(2,1)} %param.14) | copy-start | bytes 5505028
  7.2 5.3 %copy-start.8 = (s32[96,1]{0,1:T(1,128)S(1)}, s32[96,1]{0,1:T(1,128)}, u32[]{:S(2)}) copy-start(s32[96,1]{0,1:T(1,128)} %param.16) | copy-start | bytes 1156
  7.2 5.9 %copy-start.9 = (s32[96,1]{0,1:T(1,128)S(1)}, s32[96,1]{0,1:T(1,128)}, u32[]{:S(2)}) copy-start(s32[96,1]{0,1:T(1,128)} %param.17) | copy-start | bytes 1156
  7.2 74.3 %all-gather.3.cloned.1.call-start = ((), (), s32[]{:S(2)}) async-start(), calls=%async_computation.4 | async-start | bytes 4128768 | tf_op jit(solution)/shard_map/all_gather | solution.py:55
  11.9 142.5 %all-gather.5.cloned.1.call-start = ((), (), s32[]{:S(2)}) async-start(), calls=%async_computation.5 | async-start | bytes 3440640 | tf_op jit(solution)/shard_map/all_gather | solution.py:57
  87.9 37.5 %all-to-all-start = ((bf16[192,4,1024]{2,0,1:T(8,128)(2,1)}), bf16[192,4,1024]{2,0,1:T(8,128)(2,1)S(1)}, u32[]{:S(2)}, u32[]{:S(2)}) async-start(bf16[192,4,1024]{2,0,1:T(8,128)(2,1)} %bitcast.82), calls=%async_computation | async-start | bytes 3145728 | tf_op jit(solution)/shard_map/all_to_all | solution.py:44
  125.4 24.5 %all-to-all-start.2 = ((bf16[192,4,1024]{2,0,1:T(8,128)(2,1)}), bf16[192,4,1024]{2,0,1:T(8,128)(2,1)}, u32[]{:S(2)}, u32[]{:S(2)}) async-start(bf16[192,4,1024]{2,0,1:T(8,128)(2,1)} %bitcast.81), calls=%async_computation.2 | async-start | bytes 3145728 | tf_op jit(solution)/shard_map/all_to_all | solution.py:45
  129.8 233.8 %reduce-scatter.2.cloned.1.call-start = ((), (), s32[]{:S(2)}) async-start(), calls=%async_computation.6 | async-start | bytes 8257536 | tf_op jit(solution)/shard_map/reduce_scatter | solution.py:80
  159.8 1.8 copy-start.5
  159.8 2.3 copy-start.7
  165.8 1.4 copy-start.3
  169.4 1.7 copy-start.2
  218.1 4.5 %copy-start.6 = (bf16[12,128,896]{2,1,0:T(8,128)(2,1)S(1)}, bf16[12,128,896]{2,1,0:T(8,128)(2,1)}, u32[]{:S(2)}) copy-start(bf16[12,128,896]{2,1,0:T(8,128)(2,1)} %all-gather.5.cloned.1.call-done) | copy-start | bytes 8257540
  222.6 3.1 copy-start.4
  250.6 115.2 %copy-start.1 = (bf16[896,1024]{1,0:T(8,128)(2,1)S(1)}, bf16[896,1024]{1,0:T(8,128)(2,1)}, u32[]{:S(2)}) copy-start(bf16[896,1024]{1,0:T(8,128)(2,1)} %param.14) | copy-start | bytes 5505028
Sparse Core Ops, SparseCore 0:
  12.0 69.4 all-gather.2
  85.4 38.9 all-gather.4
  232.4 131.0 reduce-scatter.1
where the time goes:
time: 373 us; the launch traced here: 372 us
  waiting for transfers between devices  207 us (55%)
  matrix products  74.8 us (20%)
  local copies, waits for them, and re-layouts  35.9 us (10%)
  blocking collectives  22.7 us (6%)
  between operations  14 us (4%)
  other arithmetic  9.7 us (3%)
  starting transfers between devices  8.05 us (2%)
    reduce_scatter x1, waiting for transfers between devices, per_device(): lax.psum_scatter(jnp.concatenate([grad_key, grad_value], axis=1), 'dp', s...  89 us
    all_gather x1, waiting for transfers between devices, per_device(): pooled = lax.all_gather(owned_enc, 'dp', axis=0, tiled=True)  67.5 us
    dot_general x3, matrix products, attend(): jnp.einsum('chqk,ckhd->cqhd', weights, value_rows, preferred_element_type...  36.7 us
    all_to_all x1, waiting for transfers between devices, per_device(): lax.all_to_all(queries, 'nbr', split_axis=1, concat_axis=0, tiled=True)  30.9 us
    all_to_all x1, blocking collectives, per_device(): lax.all_to_all(attended, 'nbr', split_axis=0, concat_axis=1, tiled=True)  22.7 us
    dot_general x2, matrix products, attend(): jnp.einsum('cqhd,ckhd->chqk', shifted, key_rows, preferred_element_type=j...  19.7 us
    all_to_all x1, waiting for transfers between devices, per_device(): lax.all_to_all(cotangent, 'nbr', split_axis=1, concat_axis=0, tiled=True)  19.5 us
    unnamed x25, local copies, waits for them, and re-layouts  8.28 us
  transfers between devices with their start and end apart: 5, of which 4 were waited for; matrix products, arithmetic and copies ran while one was open for 8% of the time, Pallas kernels for 0%

commit v1 on v0

v1 whole, which is shorter than its diff:
```python
import functools

import jax
import jax.numpy as jnp
from jax import lax
from jax.experimental import pallas as pl
from jax.experimental.pallas import tpu as pltpu
from jax.sharding import PartitionSpec as P

HEAD = 128
GROUP = 64
CAP = 2
BF = jnp.bfloat16
F32 = jnp.float32


def encode(blocks, gain_vec, weight):
    widened = blocks.astype(F32)
    mean_sq = jnp.mean(widened * widened, axis=-1, keepdims=True)
    normed = (widened * lax.rsqrt(mean_sq + 1e-06) * gain_vec).astype(BF)
    combined = jnp.dot(normed, weight, preferred_element_type=F32)
    return (widened + jax.nn.gelu(combined)).astype(BF)


def pick_rows(chosen, rows, tokens):
    m, n = chosen.shape
    eye = jnp.eye(tokens, dtype=BF)
    full = chosen.astype(BF)[:, None, :, None] * eye[None, :, None, :]
    full = full.reshape(m * tokens, n * tokens)
    return jnp.dot(full, rows, preferred_element_type=F32).astype(BF)


def attention_body(q_ref, g_ref, k_ref, v_ref, o_ref, dk_ref, dv_ref):
    heads = q_ref.shape[1] // HEAD
    parts, _, tokens, _ = k_ref.shape
    keys = parts * tokens
    scale = HEAD ** (-0.5)
    over_last = (((1,), (1,)), ((), ()))
    over_first = (((0,), (0,)), ((), ()))
    for h in range(heads):
        cols = slice(h * HEAD, (h + 1) * HEAD)
        q = q_ref[:, cols]
        g = g_ref[:, cols]
        k = k_ref[:, 0, :, cols].reshape(keys, HEAD)
        v = v_ref[:, 0, :, cols].reshape(keys, HEAD)
        s = lax.dot_general(q, k, over_last, preferred_element_type=F32) * scale
        e = jnp.exp(s - jnp.max(s, axis=-1, keepdims=True))
        p = e / jnp.sum(e, axis=-1, keepdims=True)
        w = p.astype(BF)
        o_ref[:, cols] = jnp.dot(w, v, preferred_element_type=F32).astype(BF)
        dw = lax.dot_general(g, v, over_last, preferred_element_type=F32)
        dw = dw.astype(BF).astype(F32)
        ds = p * (dw - jnp.sum(dw * p, axis=-1, keepdims=True)) * scale
        dk = lax.dot_general(ds.astype(BF), q, over_first, preferred_element_type=F32)
        dv = lax.dot_general(w, g, over_first, preferred_element_type=F32)
        dk_ref[:, 0, :, cols] = dk.astype(BF).reshape(parts, tokens, HEAD)
        dv_ref[:, 0, :, cols] = dv.astype(BF).reshape(parts, tokens, HEAD)


def attention(q, g, k, v):
    length, width = q.shape
    parts, groups, tokens, _ = k.shape
    row = pl.BlockSpec((GROUP, width), lambda c: (c, 0))
    block = pl.BlockSpec((parts, 1, tokens, width), lambda c: (0, c, 0, 0))
    work = 10 * length * parts * tokens * width
    return pl.pallas_call(
        attention_body,
        grid=(groups,),
        in_specs=[row, row, block, block],
        out_specs=[row, block, block],
        out_shape=[
            jax.ShapeDtypeStruct(q.shape, BF),
            jax.ShapeDtypeStruct(k.shape, BF),
            jax.ShapeDtypeStruct(v.shape, BF),
        ],
        compiler_params=pltpu.CompilerParams(vmem_limit_bytes=32 * 2**20),
        cost_estimate=pl.CostEstimate(
            flops=work,
            bytes_accessed=6 * length * width + 8 * k.size,
            transcendentals=length * parts * tokens * width // HEAD,
        ),
    )(q, g, k, v)


def per_device(
    queries, cotangent, pool, enc_gain, enc_weight, k_weight, v_weight, nbr_owner, nbr_slot
):
    dp_count = lax.axis_size("dp")
    nbr_count = lax.axis_size("nbr")
    me = lax.axis_index("dp")
    held, tokens, enc_width = pool.shape
    per_row = nbr_owner.shape[0] // dp_count

    owners = nbr_owner[:, 0].reshape(dp_count, per_row)
    slots = nbr_slot[:, 0].reshape(dp_count, per_row)
    same = owners[:, :, None] == owners[:, None, :]
    earlier = jnp.tril(jnp.ones((per_row, per_row), jnp.bool_), -1)
    rank = jnp.sum((same & earlier[None]).astype(jnp.int32), axis=-1)

    ranks = jnp.arange(CAP, dtype=jnp.int32)
    blocks = jnp.arange(held, dtype=jnp.int32)
    mine = (owners == me)[:, None, :] & (rank[:, None, :] == ranks[None, :, None])
    send = jnp.any(
        mine[:, :, None, :] & (slots[:, None, None, :] == blocks[None, None, :, None]), axis=-1
    ).reshape(dp_count * CAP, held)
    enc = encode(pool.reshape(held * tokens, enc_width), enc_gain, enc_weight)
    outgoing = pick_rows(send, enc, tokens)
    arrived = lax.all_to_all(outgoing, "dp", split_axis=0, concat_axis=0, tiled=True)

    place = lax.dynamic_slice_in_dim(owners * CAP + rank, me, 1, 0)[0]
    take = place[:, None] == jnp.arange(dp_count * CAP, dtype=jnp.int32)[None, :]
    picked = pick_rows(take, arrived, tokens)
    flat_enc = lax.all_gather(picked, "nbr", axis=0, tiled=True)

    q_rows = lax.all_to_all(queries, "nbr", split_axis=1, concat_axis=0, tiled=True)
    g_rows = lax.all_to_all(cotangent, "nbr", split_axis=1, concat_axis=0, tiled=True)
    seq_len, width = q_rows.shape
    lead = GROUP - 1
    blank = jnp.zeros((lead, width), BF)
    q_rows = jnp.concatenate([q_rows[lead:], blank], axis=0)
    g_rows = jnp.concatenate([g_rows[lead:], blank], axis=0)

    shape4 = (nbr_count, per_row, tokens, width)
    keys = jnp.dot(flat_enc, k_weight, preferred_element_type=F32).astype(BF)
    values = jnp.dot(flat_enc, v_weight, preferred_element_type=F32).astype(BF)
    out, dk, dv = attention(q_rows, g_rows, keys.reshape(shape4), values.reshape(shape4))

    over_first = (((0,), (0,)), ((), ()))

    def weight_grad(grads):
        product = lax.dot_general(
            flat_enc, grads.reshape(-1, width), over_first, preferred_element_type=F32
        )
        return lax.psum_scatter(
            product.astype(BF), "dp", scatter_dimension=0, tiled=True
        ).astype(F32)

    grad_v = weight_grad(dv)
    grad_k = weight_grad(dk)
    out = jnp.concatenate([blank, out[: seq_len - lead]], axis=0)
    merged = lax.all_to_all(out, "nbr", split_axis=0, concat_axis=1, tiled=True)
    return (merged, grad_k, grad_v)


def solution(mesh):
    return jax.shard_map(
        per_device,
        mesh=mesh,
        in_specs=(
            P(("dp", "nbr"), None),
            P(("dp", "nbr"), None),
            P("dp", "nbr", None),
            P(),
            P(),
            P(None, "nbr"),
            P(None, "nbr"),
            P(),
            P(),
        ),
        out_specs=(P(("dp", "nbr"), None), P("dp", "nbr"), P("dp", "nbr")),
        check_vma=False,
    )
```

time: 373 us -> 318 us (0.85)
  matrix products: 74.8 us -> 26.8 us
  Pallas kernels: 0 us -> 41.5 us
  waiting for transfers between devices: 207 us -> 169 us
  local copies, waits for them, and re-layouts: 35.9 us -> 19.4 us
  starting transfers between devices: 8.05 us -> 15.5 us
    all_gather x2 -> x1, waiting for transfers between devices: 67.5 us -> 0.01 us  [per_device(): flat_enc = lax.all_gather(picked, 'nbr', axis=0, tiled=True)]
    dot_general x10 -> x7, matrix products: 74.8 us -> 26.8 us  [the longest x2 11.3 us: weight_grad(): lax.dot_general(flat_enc, grads.reshape(-1, width), over_first, preferred...]
    pallas_call x0 -> x1, Pallas kernels: none -> 41.5 us  [attention(): pl.pallas_call(attention_body, grid=(groups,), in_specs=[row, row, block,...]
    all_to_all x0 -> x1, waiting for transfers between devices: none -> 20.4 us  [per_device(): lax.all_to_all(outgoing, 'dp', split_axis=0, concat_axis=0, tiled=True)]
    convert_element_type x3 -> x0, local copies, waits for them, and re-layouts: 12 us -> none  [the longest x1 4.84 us: attend(): jnp.einsum('chqk,ckhd->cqhd', weights, value_rows, preferred_element_type...]
    reduce_scatter x1 -> x2, waiting for transfers between devices: 89 us -> 97.9 us  [weight_grad(): lax.psum_scatter(product.astype(BF), 'dp', scatter_dimension=0, tiled=True)]
    all_to_all x0 -> x1, starting transfers between devices: none -> 7.27 us  [per_device(): lax.all_to_all(outgoing, 'dp', split_axis=0, concat_axis=0, tiled=True)]
    convert_element_type x0 -> x6, other arithmetic: none -> 3.76 us  [the longest x2 3.49 us: weight_grad(): return lax.psum_scatter(product.astype(BF), 'dp', scatter_dimension=0, ti...]
  transfers between devices with their start and end apart: 5 -> 6, of which waited for: 4 -> 5; matrix products, arithmetic and copies ran while one was open for 8% -> 7% of each run, Pallas kernels for 0% -> 0%
where the time goes in v1:
time: 318 us
  waiting for transfers between devices  169 us (53%)
  Pallas kernels  41.5 us (13%)
  matrix products  26.8 us (8%)
  blocking collectives  22.5 us (7%)
  local copies, waits for them, and re-layouts  19.4 us (6%)
  starting transfers between devices  15.5 us (5%)
  between operations  14 us (4%)
  other arithmetic  8.93 us (3%)
    reduce_scatter x2, waiting for transfers between devices, weight_grad(): lax.psum_scatter(product.astype(BF), 'dp', scatter_dimension=0, tiled=True)  97.9 us
    pallas_call x1, Pallas kernels, attention(): pl.pallas_call(attention_body, grid=(groups,), in_specs=[row, row, block,...  41.5 us
    all_to_all x1, waiting for transfers between devices, per_device(): lax.all_to_all(queries, 'nbr', split_axis=1, concat_axis=0, tiled=True)  31.9 us
    all_to_all x1, blocking collectives, per_device(): merged = lax.all_to_all(out, 'nbr', split_axis=0, concat_axis=1, tiled=True)  22.5 us
    all_to_all x1, waiting for transfers between devices, per_device(): lax.all_to_all(outgoing, 'dp', split_axis=0, concat_axis=0, tiled=True)  20.4 us
    all_to_all x1, waiting for transfers between devices, per_device(): lax.all_to_all(cotangent, 'nbr', split_axis=1, concat_axis=0, tiled=True)  18.6 us
    dot_general x2, matrix products, weight_grad(): lax.dot_general(flat_enc, grads.reshape(-1, width), over_first, preferred...  11.3 us
    all_to_all x1, starting transfers between devices, per_device(): lax.all_to_all(outgoing, 'dp', split_axis=0, concat_axis=0, tiled=True)  7.27 us
  transfers between devices with their start and end apart: 6, of which 5 were waited for; matrix products, arithmetic and copies ran while one was open for 7% of the time, Pallas kernels for 0%

profile of v1, /device:TPU:0, one launch (start us, length us, event | category | flops | bytes accessed | tf_op | source)
XLA Modules:
  0.0 317.6 jit_solution(8046879766560499472)
XLA Ops:
  7.2 0.5 broadcast.83
  7.7 1.3 reduce.9
  9.1 1.3 reduce.10
  10.5 0.1 reshape_squeeze.3
  10.6 0.1 copy.23
  10.7 1.2 fusion.9
  11.9 0.1 rsqrt.12
  12.0 0.3 convert_reduce_fusion
  12.4 0.1 copy.25
  12.5 0.4 and_reduce_fusion
  12.9 0.1 broadcast_multiply_fusion.1
  13.0 1.4 mul.96
  14.4 0.2 fusion.11
  14.6 2.2 fusion.8
  16.9 1.4 convolution_convert_fusion.4
  18.3 7.3 %all-to-all-start.2 = ((bf16[8,64,896]{2,1,0:T(8,128)(2,1)}), bf16[8,64,896]{2,1,0:T(8,128)(2,1)}, u32[]{:S(2)}, u32[]{:S(2)}) async-start(bf16[8,64,896]{2,1,0:T(8,128)(2,1)} %bitcast.6), calls=%async_computation.2 | async-start | bytes 1835008 | tf_op jit(solution)/shard_map/all_to_all | solution.py:108
  25.6 0.2 fusion.13
  25.9 0.2 broadcast_multiply_fusion
  26.0 2.3 mul.92
  28.3 20.4 %all-to-all-done.2 = bf16[8,64,896]{2,1,0:T(8,128)(2,1)} async-done(((bf16[8,64,896]{2,1,0:T(8,128)(2,1)}), bf16[8,64,896]{2,1,0:T(8,128)(2,1)}, u32[]{:S(2)}, u32[]{:S(2)}) %all-to-all-start.2) | async-done | bytes 917536 | tf_op jit(solution)/shard_map/all_to_all | solution.py:108
  48.7 2.7 convolution_convert_fusion.5
  51.4 1.3 copy.33
  52.7 3.6 %all-to-all-start = ((bf16[192,4,1024]{2,0,1:T(8,128)(2,1)}), bf16[192,4,1024]{2,0,1:T(8,128)(2,1)S(1)}, u32[]{:S(2)}, u32[]{:S(2)}) async-start(bf16[192,4,1024]{2,0,1:T(8,128)(2,1)} %bitcast.51), calls=%async_computation | async-start | bytes 3145728 | tf_op jit(solution)/shard_map/all_to_all | solution.py:115
  56.3 2.8 copy.32
  59.2 31.9 %all-to-all-done = bf16[192,4,1024]{2,0,1:T(8,128)(2,1)S(1)} async-done(((bf16[192,4,1024]{2,0,1:T(8,128)(2,1)}), bf16[192,4,1024]{2,0,1:T(8,128)(2,1)S(1)}, u32[]{:S(2)}, u32[]{:S(2)}) %all-to-all-start) | async-done | bytes 1572896 | tf_op jit(solution)/shard_map/all_to_all | solution.py:115
  91.1 4.3 %all-to-all-start.1 = ((bf16[192,4,1024]{2,0,1:T(8,128)(2,1)}), bf16[192,4,1024]{2,0,1:T(8,128)(2,1)}, u32[]{:S(2)}, u32[]{:S(2)}) async-start(bf16[192,4,1024]{2,0,1:T(8,128)(2,1)} %bitcast.50), calls=%async_computation.1 | async-start | bytes 3145728 | tf_op jit(solution)/shard_map/all_to_all | solution.py:116
  95.5 1.5 slice.12
  97.0 18.6 %all-to-all-done.1 = bf16[192,4,1024]{2,0,1:T(8,128)(2,1)} async-done(((bf16[192,4,1024]{2,0,1:T(8,128)(2,1)}), bf16[192,4,1024]{2,0,1:T(8,128)(2,1)}, u32[]{:S(2)}, u32[]{:S(2)}) %all-to-all-start.1) | async-done | bytes 1572896 | tf_op jit(solution)/shard_map/all_to_all | solution.py:116
  115.6 1.8 slice.13
  117.4 0.1 concatenate.9.q_ref
  117.6 1.3 concatenate.10.g_ref
  118.9 5.6 %convolution_convert_fusion = bf16[1536,1024]{1,0:T(8,128)(2,1)S(1)} fusion(bf16[1536,896]{1,0:T(8,128)(2,1)} %all-gather.2.cloned.1.call-done, bf16[896,1024]{1,0:T(8,128)(2,1)S(1)} %copy-done), kind=kOutput, calls=%fused_computation | convolution fusion | flops 2820145152 | bytes 7733248 | tf_op jit(solution)/shard_map/dot_general | solution.py:125
  124.5 3.6 %convolution_convert_fusion.1 = bf16[1536,1024]{1,0:T(8,128)(2,1)S(1)} fusion(bf16[1536,896]{1,0:T(8,128)(2,1)S(1)} %copy-done.10, bf16[896,1024]{1,0:T(8,128)(2,1)S(1)} %copy-done.11), kind=kOutput, calls=%fused_computation.1 | convolution fusion | flops 2820145152 | bytes 7733248 | tf_op jit(solution)/shard_map/dot_general | solution.py:124
  128.1 41.5 %shard_map.112 = (bf16[768,1024]{1,0:T(8,128)(2,1)S(1)}, bf16[4,12,32,1024]{3,2,1,0:T(8,128)(2,1)S(1)}, bf16[4,12,32,1024]{3,2,1,0:T(8,128)(2,1)S(1)}) custom-call(bf16[768,1024]{1,0:T(8,128)(2,1)S(1)} %concatenate.9.q_ref, bf16[768,1024]{1,0:T(8,128)(2,1)S(1)} %copy-done.1, bf16[4,12,32,1024]{3,2,1,0:T(8,128)(2,1)S(1)} %bitcast.53, ...), custom_call_target="tpu_custom_call" | custom-call | flops 1006632960 | bytes 17301504 | tf_op jit(solution)/shard_map/pallas_call | solution.py:66
  169.6 1.1 copy-done.2
  170.7 1.6 copy-done.4
  172.4 4.2 %convolution_convert_fusion.3 = bf16[896,1024]{1,0:T(8,128)(2,1)} fusion(bf16[1536,896]{1,0:T(8,128)(2,1)S(1)} %copy-done.10, bf16[1536,1024]{1,0:T(8,128)(2,1)S(1)} %bitcast.55), kind=kOutput, calls=%fused_computation.3 | convolution fusion | flops 2819489792 | bytes 7733248 | tf_op jit(solution)/shard_map/dot_general | solution.py:131
  176.6 0.2 reduce-scatter.5.cloned.1.call-start
  176.9 7.1 %convolution_convert_fusion.2 = bf16[896,1024]{1,0:T(8,128)(2,1)} fusion(bf16[1536,896]{1,0:T(8,128)(2,1)} %all-gather.2.cloned.1.call-done, bf16[1536,1024]{1,0:T(8,128)(2,1)} %bitcast.54), kind=kOutput, calls=%fused_computation.2 | convolution fusion | flops 2819489792 | bytes 7733248 | tf_op jit(solution)/shard_map/dot_general | solution.py:131
  184.0 1.4 copy-done.3
  185.4 0.1 slice.11
  185.5 0.4 concatenate.11
  185.9 22.5 %all_to_all.69 = bf16[4,192,1024]{2,1,0:T(8,128)(2,1)S(1)} all-to-all(bf16[4,192,1024]{2,1,0:T(8,128)(2,1)S(1)} %bitcast.56), channel_id=1, replica_groups=mesh['dp'=8,'nbr'=4] {'nbr'}, dimensions={0} | all-to-all | bytes 3145728 | tf_op jit(solution)/shard_map/all_to_all | solution.py:141
  208.4 1.3 copy.29
  209.7 30.9 %reduce-scatter.3.cloned.1.call-done = bf16[112,1024]{1,0:T(8,128)(2,1)} async-done(((bf16[896,1024]{1,0:T(8,128)(2,1)}), bf16[112,1024]{1,0:T(8,128)(2,1)}) %reduce-scatter.3.cloned.1.call-update) | async-done | bytes 229392 | tf_op jit(solution)/shard_map/reduce_scatter | solution.py:134
  240.6 1.7 convert_element_type.84
  242.3 67.0 %reduce-scatter.5.cloned.1.call-done = bf16[112,1024]{1,0:T(8,128)(2,1)} async-done(((bf16[896,1024]{1,0:T(8,128)(2,1)}), bf16[112,1024]{1,0:T(8,128)(2,1)}) %reduce-scatter.5.cloned.1.call-update) | async-done | bytes 229392 | tf_op jit(solution)/shard_map/reduce_scatter | solution.py:134
  309.3 1.7 convert_element_type.86
  (37 shorter events, 0.5 us)
Async XLA Ops:
  7.2 111.7 %copy-start = (bf16[896,1024]{1,0:T(8,128)(2,1)S(1)}, bf16[896,1024]{1,0:T(8,128)(2,1)}, u32[]{:S(2)}) copy-start(bf16[896,1024]{1,0:T(8,128)(2,1)} %param.15) | copy-start | bytes 5505028
  7.2 7.3 %copy-start.6 = (bf16[8,32,896]{2,1,0:T(8,128)(2,1)S(1)}, bf16[8,32,896]{2,1,0:T(8,128)(2,1)}, u32[]{:S(2)}) copy-start(bf16[8,32,896]{2,1,0:T(8,128)(2,1)} %param.11) | copy-start | bytes 1376260
  7.2 7.3 %copy-start.9 = (f32[896]{0:T(1024)S(1)}, f32[896]{0:T(1024)}, u32[]{:S(2)}) copy-start(f32[896]{0:T(1024)} %param.12) | copy-start | bytes 10756
  14.6 2.3 copy-start.8
  18.3 30.4 %all-to-all-start.2 = ((bf16[8,64,896]{2,1,0:T(8,128)(2,1)}), bf16[8,64,896]{2,1,0:T(8,128)(2,1)}, u32[]{:S(2)}, u32[]{:S(2)}) async-start(bf16[8,64,896]{2,1,0:T(8,128)(2,1)} %bitcast.6), calls=%async_computation.2 | async-start | bytes 1835008 | tf_op jit(solution)/shard_map/all_to_all | solution.py:108
  25.5 93.3 %all-gather.2.cloned.1.call-start = ((), (), s32[]{:S(2)}) async-start(), calls=%async_computation.6 | async-start | bytes 3440640 | tf_op jit(solution)/shard_map/all_gather | solution.py:113
  28.3 23.1 %copy-start.7 = (bf16[192,4096]{1,0:T(8,128)(2,1)S(1)}, bf16[192,4096]{1,0:T(8,128)(2,1)}, u32[]{:S(2)}) copy-start(bf16[192,4096]{1,0:T(8,128)(2,1)} %param.9) | copy-start | bytes 4718596
  52.7 38.4 %all-to-all-start = ((bf16[192,4,1024]{2,0,1:T(8,128)(2,1)}), bf16[192,4,1024]{2,0,1:T(8,128)(2,1)S(1)}, u32[]{:S(2)}, u32[]{:S(2)}) async-start(bf16[192,4,1024]{2,0,1:T(8,128)(2,1)} %bitcast.51), calls=%async_computation | async-start | bytes 3145728 | tf_op jit(solution)/shard_map/all_to_all | solution.py:115
  91.1 24.5 %all-to-all-start.1 = ((bf16[192,4,1024]{2,0,1:T(8,128)(2,1)}), bf16[192,4,1024]{2,0,1:T(8,128)(2,1)}, u32[]{:S(2)}, u32[]{:S(2)}) async-start(bf16[192,4,1024]{2,0,1:T(8,128)(2,1)} %bitcast.50), calls=%async_computation.1 | async-start | bytes 3145728 | tf_op jit(solution)/shard_map/all_to_all | solution.py:116
  95.5 145.1 %reduce-scatter.3.cloned.1.call-start = ((), (), s32[]{:S(2)}) async-start(), calls=%async_computation.7 | async-start | bytes 2064384 | tf_op jit(solution)/shard_map/reduce_scatter | solution.py:134
  115.6 1.8 copy-start.5
  118.9 5.6 %copy-start.10 = (bf16[1536,896]{1,0:T(8,128)(2,1)S(1)}, bf16[1536,896]{1,0:T(8,128)(2,1)}, u32[]{:S(2)}) copy-start(bf16[1536,896]{1,0:T(8,128)(2,1)} %all-gather.2.cloned.1.call-done) | copy-start | bytes 8257540
  118.9 5.6 %copy-start.11 = (bf16[896,1024]{1,0:T(8,128)(2,1)S(1)}, bf16[896,1024]{1,0:T(8,128)(2,1)}, u32[]{:S(2)}) copy-start(bf16[896,1024]{1,0:T(8,128)(2,1)} %param.14) | copy-start | bytes 5505028
  124.5 3.6 %copy-start.1 = (bf16[768,1024]{1,0:T(8,128)(2,1)S(1)}, bf16[768,1024]{1,0:T(8,128)(2,1)}, u32[]{:S(2)}) copy-start(bf16[768,1024]{1,0:T(8,128)(2,1)} %concatenate.10.g_ref) | copy-start | bytes 4718596
  169.6 1.1 copy-start.2
  170.7 1.6 copy-start.4
  176.6 132.7 %reduce-scatter.5.cloned.1.call-start = ((), (), s32[]{:S(2)}) async-start(), calls=%async_computation.8 | async-start | bytes 2064384 | tf_op jit(solution)/shard_map/reduce_scatter | solution.py:134
  183.9 1.4 copy-start.3
Sparse Core Ops, SparseCore 0:
  51.6 39.9 all-gather.1
  176.7 63.7 reduce-scatter.2
  244.4 64.8 reduce-scatter.4

commit v2 on v1

--- a/solution.py
+++ b/solution.py
@@ -1,5 +1,3 @@
-import functools
-
 import jax
 import jax.numpy as jnp
 from jax import lax
@@ -37,24 +35,28 @@
     scale = HEAD ** (-0.5)
     over_last = (((1,), (1,)), ((), ()))
     over_first = (((0,), (0,)), ((), ()))
-    for h in range(heads):
-        cols = slice(h * HEAD, (h + 1) * HEAD)
-        q = q_ref[:, cols]
-        g = g_ref[:, cols]
-        k = k_ref[:, 0, :, cols].reshape(keys, HEAD)
-        v = v_ref[:, 0, :, cols].reshape(keys, HEAD)
-        s = lax.dot_general(q, k, over_last, preferred_element_type=F32) * scale
-        e = jnp.exp(s - jnp.max(s, axis=-1, keepdims=True))
-        p = e / jnp.sum(e, axis=-1, keepdims=True)
-        w = p.astype(BF)
-        o_ref[:, cols] = jnp.dot(w, v, preferred_element_type=F32).astype(BF)
-        dw = lax.dot_general(g, v, over_last, preferred_element_type=F32)
-        dw = dw.astype(BF).astype(F32)
-        ds = p * (dw - jnp.sum(dw * p, axis=-1, keepdims=True)) * scale
-        dk = lax.dot_general(ds.astype(BF), q, over_first, preferred_element_type=F32)
-        dv = lax.dot_general(w, g, over_first, preferred_element_type=F32)
-        dk_ref[:, 0, :, cols] = dk.astype(BF).reshape(parts, tokens, HEAD)
-        dv_ref[:, 0, :, cols] = dv.astype(BF).reshape(parts, tokens, HEAD)
+    for first in range(0, heads, 4):
+        held = []
+        for h in range(first, min(first + 4, heads)):
+            cols = slice(h * HEAD, (h + 1) * HEAD)
+            k = k_ref[:, 0, :, cols].reshape(keys, HEAD)
+            v = v_ref[:, 0, :, cols].reshape(keys, HEAD)
+            s = lax.dot_general(q_ref[:, cols], k, over_last, preferred_element_type=F32)
+            dw = lax.dot_general(g_ref[:, cols], v, over_last, preferred_element_type=F32)
+            held.append((cols, v, s * scale, dw.astype(BF).astype(F32)))
+        ready = []
+        for cols, v, s, dw in held:
+            e = jnp.exp(s - jnp.max(s, axis=-1, keepdims=True))
+            p = e * (1.0 / jnp.sum(e, axis=-1, keepdims=True))
+            ds = p * (dw - jnp.sum(dw * p, axis=-1, keepdims=True)) * scale
+            ready.append((cols, v, p.astype(BF), ds.astype(BF)))
+        for cols, v, w, ds in ready:
+            q, g = q_ref[:, cols], g_ref[:, cols]
+            o_ref[:, cols] = jnp.dot(w, v, preferred_element_type=F32).astype(BF)
+            dk = lax.dot_general(ds, q, over_first, preferred_element_type=F32)
+            dv = lax.dot_general(w, g, over_first, preferred_element_type=F32)
+            dk_ref[:, 0, :, cols] = dk.astype(BF).reshape(parts, tokens, HEAD)
+            dv_ref[:, 0, :, cols] = dv.astype(BF).reshape(parts, tokens, HEAD)
 
 
 def attention(q, g, k, v):
@@ -82,6 +84,44 @@
     )(q, g, k, v)
 
 
+def exchange(x, axis, split, join):
+    n = lax.axis_size(axis)
+    me = lax.axis_index(axis)
+    span = x.shape[split] // n
+    step = x.shape[join]
+    parts = []
+    for d in range(n):
+        piece = lax.dynamic_slice_in_dim(x, (me ^ d) * span, span, split)
+        if d:
+            piece = lax.ppermute(piece, axis, [(i, i ^ d) for i in range(n)])
+        parts.append(piece)
+    shape = list(parts[0].shape)
+    shape[join] = n * step
+    whole = jnp.zeros(shape, x.dtype)
+    for d, piece in enumerate(parts):
+        whole = lax.dynamic_update_slice_in_dim(whole, piece, (me ^ d) * step, join)
+    return whole
+
+
+def halving(total, axis, turn):
+    n = lax.axis_size(axis)
+    me = lax.axis_index(axis)
+    count = n.bit_length() - 1
+    bits = [(i + turn) % count for i in range(count)]
+    rows, width = total.shape
+    current = total.reshape((2,) * count + (rows // n, width))
+    left = list(range(count - 1, -1, -1))
+    for bit in bits:
+        place = left.index(bit)
+        left.pop(place)
+        mine = (me >> bit) & 1
+        away = lax.dynamic_index_in_dim(current, 1 - mine, place, keepdims=False)
+        keep = lax.dynamic_index_in_dim(current, mine, place, keepdims=False)
+        pairs = [(i, i ^ (1 << bit)) for i in range(n)]
+        current = keep + lax.ppermute(away.astype(BF), axis, pairs).astype(F32)
+    return current
+
+
 def per_device(
     queries, cotangent, pool, enc_gain, enc_weight, k_weight, v_weight, nbr_owner, nbr_slot
 ):
@@ -112,8 +152,8 @@
     picked = pick_rows(take, arrived, tokens)
     flat_enc = lax.all_gather(picked, "nbr", axis=0, tiled=True)
 
-    q_rows = lax.all_to_all(queries, "nbr", split_axis=1, concat_axis=0, tiled=True)
-    g_rows = lax.all_to_all(cotangent, "nbr", split_axis=1, concat_axis=0, tiled=True)
+    q_rows = exchange(queries, "nbr", 1, 0)
+    g_rows = exchange(cotangent, "nbr", 1, 0)
     seq_len, width = q_rows.shape
     lead = GROUP - 1
     blank = jnp.zeros((lead, width), BF)
@@ -127,18 +167,16 @@
 
     over_first = (((0,), (0,)), ((), ()))
 
-    def weight_grad(grads):
+    def weight_grad(grads, turn):
         product = lax.dot_general(
             flat_enc, grads.reshape(-1, width), over_first, preferred_element_type=F32
         )
-        return lax.psum_scatter(
-            product.astype(BF), "dp", scatter_dimension=0, tiled=True
-        ).astype(F32)
-
-    grad_v = weight_grad(dv)
-    grad_k = weight_grad(dk)
+        return halving(product, "dp", turn)
+
+    grad_v = weight_grad(dv, 0)
+    grad_k = weight_grad(dk, 1)
     out = jnp.concatenate([blank, out[: seq_len - lead]], axis=0)
-    merged = lax.all_to_all(out, "nbr", split_axis=0, concat_axis=1, tiled=True)
+    merged = exchange(out, "nbr", 0, 1)
     return (merged, grad_k, grad_v)
 
 

time: 318 us -> 226 us (0.71)
  waiting for transfers between devices: 169 us -> 113 us
  Pallas kernels: 41.5 us -> 17.6 us
  blocking collectives: 22.5 us -> 0 us
  local copies, waits for them, and re-layouts: 19.4 us -> 30.5 us
  matrix products: 26.8 us -> 21.5 us
    reduce_scatter x2 -> x0, waiting for transfers between devices: 97.9 us -> none  [weight_grad(): lax.psum_scatter(product.astype(BF), 'dp', scatter_dimension=0, tiled=True)]
    ppermute x0 -> x15, waiting for transfers between devices: none -> 92.8 us  [the longest x9 49 us: exchange(): piece = lax.ppermute(piece, axis, [(i, i ^ d) for i in range(n)])]
    all_to_all x2 -> x0, waiting for transfers between devices: 50.6 us -> none  [the longest x1 31.9 us: per_device(): lax.all_to_all(queries, 'nbr', split_axis=1, concat_axis=0, tiled=True)]
    pallas_call x1, Pallas kernels: 41.5 us -> 17.6 us  [attention(): pl.pallas_call(attention_body, grid=(groups,), in_specs=[row, row, block,...]
    all_to_all x1 -> x0, blocking collectives: 22.5 us -> none  [per_device(): merged = lax.all_to_all(out, 'nbr', split_axis=0, concat_axis=1, tiled=True)]
    ppermute x0 -> x15, starting transfers between devices: none -> 10.9 us  [the longest x9 7.32 us: exchange(): piece = lax.ppermute(piece, axis, [(i, i ^ d) for i in range(n)])]
    all_to_all x2 -> x0, starting transfers between devices: 7.91 us -> none  [the longest x1 4.34 us: per_device(): lax.all_to_all(cotangent, 'nbr', split_axis=1, concat_axis=0, tiled=True)]
    dynamic_update_slice x0 -> x8, local copies, waits for them, and re-layouts: none -> 7.48 us  [exchange(): whole = lax.dynamic_update_slice_in_dim(whole, piece, (me ^ d) * step, join)]
  transfers between devices with their start and end apart: 6 -> 17, of which waited for: 5 -> 12; matrix products, arithmetic and copies ran while one was open for 7% -> 13% of each run, Pallas kernels for 0% -> 0%
where the time goes in v2:
time: 226 us
  waiting for transfers between devices  113 us (50%)
  local copies, waits for them, and re-layouts  30.5 us (13%)
  matrix products  21.5 us (10%)
  starting transfers between devices  18.2 us (8%)
  Pallas kernels  17.6 us (8%)
  between operations  14.5 us (6%)
  other arithmetic  10.2 us (5%)
    ppermute x9, waiting for transfers between devices, exchange(): piece = lax.ppermute(piece, axis, [(i, i ^ d) for i in range(n)])  49 us
    ppermute x6, waiting for transfers between devices, halving(): current = keep + lax.ppermute(away.astype(BF), axis, pairs).astype(F32)  43.8 us
    all_to_all x1, waiting for transfers between devices, per_device(): lax.all_to_all(outgoing, 'dp', split_axis=0, concat_axis=0, tiled=True)  20.4 us
    pallas_call x1, Pallas kernels, attention(): pl.pallas_call(attention_body, grid=(groups,), in_specs=[row, row, block,...  17.6 us
    dynamic_update_slice x8, local copies, waits for them, and re-layouts, exchange(): whole = lax.dynamic_update_slice_in_dim(whole, piece, (me ^ d) * step, join)  7.48 us
    ppermute x9, starting transfers between devices, exchange(): piece = lax.ppermute(piece, axis, [(i, i ^ d) for i in range(n)])  7.32 us
    all_to_all x1, starting transfers between devices, per_device(): lax.all_to_all(outgoing, 'dp', split_axis=0, concat_axis=0, tiled=True)  7.28 us
    dot_general x2, matrix products, weight_grad(): lax.dot_general(flat_enc, grads.reshape(-1, width), over_first, preferred...  6 us
  transfers between devices with their start and end apart: 17, of which 12 were waited for; matrix products, arithmetic and copies ran while one was open for 13% of the time, Pallas kernels for 0%

profile of v2, /device:TPU:0, one launch (start us, length us, event | category | flops | bytes accessed | tf_op | source)
XLA Modules:
  0.0 225.7 jit_solution(521196433872474045)
XLA Ops:
  7.7 1.3 reduce.9
  9.8 1.3 reduce.10
  11.7 1.4 mul.144
  13.6 2.2 fusion.8
  15.9 1.4 convolution_convert_fusion.2
  17.3 7.3 %all-to-all-start = ((bf16[8,64,896]{2,1,0:T(8,128)(2,1)}), bf16[8,64,896]{2,1,0:T(8,128)(2,1)}, u32[]{:S(2)}, u32[]{:S(2)}) async-start(bf16[8,64,896]{2,1,0:T(8,128)(2,1)} %bitcast.2), calls=%async_computation | async-start | bytes 1835008 | tf_op jit(solution)/shard_map/all_to_all | solution.py:148
  25.0 2.3 mul.140
  27.3 20.4 %all-to-all-done = bf16[8,64,896]{2,1,0:T(8,128)(2,1)} async-done(((bf16[8,64,896]{2,1,0:T(8,128)(2,1)}), bf16[8,64,896]{2,1,0:T(8,128)(2,1)}, u32[]{:S(2)}, u32[]{:S(2)}) %all-to-all-start) | async-done | bytes 917536 | tf_op jit(solution)/shard_map/all_to_all | solution.py:148
  47.7 2.7 %convolution_convert_fusion.3 = bf16[384,896]{1,0:T(8,128)(2,1)} fusion(bf16[384,512]{1,0:T(8,128)(2,1)} %mul.140, bf16[512,896]{1,0:T(8,128)(2,1)} %bitcast.3), kind=kOutput, calls=%fused_computation.8 | convolution fusion | flops 352665600 | bytes 1998848 | tf_op jit(solution)/shard_map/dot_general | solution.py:28
  50.7 2.5 %constant_dynamic-slice_fusion.5 = (bf16[192,1024]{1,0:T(8,128)(2,1)}, bf16[192,1024]{1,0:T(8,128)(2,1)}, bf16[768,1024]{1,0:T(8,128)(2,1)S(1)}, bf16[192,1024]{1,0:T(8,128)(2,1)}) fusion(bf16[192,4096]{1,0:T(8,128)(2,1)} %param.9, s32[]{:T(128)S(6)} %select_n.80, s32[]{:T(128)S(6)} %select_n.76, bf16[768,1024]{1,0:T(8,128)(2,1)S(1)} %broadcast.79.clone.1, ...), kind=kLoop, calls=%fused_computation.64 | loop fusion | bytes 3145748 | tf_op jit(solution)/shard_map/dynamic_slice | solution.py:94
  53.2 1.3 broadcast.79.clone
  54.5 1.2 constant_dynamic-slice_fusion.1
  56.2 1.5 collective-permute-start.1
  58.8 1.2 collective-permute-start.5
  60.0 1.0 constant_dynamic-update-slice_fusion.8
  61.0 1.8 constant_dynamic-update-slice_fusion.5
  62.8 13.7 %collective-permute-done.1 = bf16[192,1024]{1,0:T(8,128)(2,1)} collective-permute-done((bf16[192,1024]{1,0:T(8,128)(2,1)}, bf16[192,1024]{1,0:T(8,128)(2,1)}, u32[]{:S(2)}, u32[]{:S(2)}) %collective-permute-start.1) | collective-permute-done | bytes 393248 | tf_op jit(solution)/shard_map/ppermute | solution.py:96
  76.5 1.0 constant_dynamic-update-slice_fusion.7
  77.5 13.7 %collective-permute-done.4 = bf16[192,1024]{1,0:T(8,128)(2,1)} collective-permute-done((bf16[192,1024]{1,0:T(8,128)(2,1)}, bf16[192,1024]{1,0:T(8,128)(2,1)}, u32[]{:S(2)}, u32[]{:S(2)}) %collective-permute-start.4) | collective-permute-done | bytes 393248 | tf_op jit(solution)/shard_map/ppermute | solution.py:96
  91.2 1.8 constant_dynamic-update-slice_fusion.4
  93.0 5.7 %collective-permute-done.2 = bf16[192,1024]{1,0:T(8,128)(2,1)} collective-permute-done((bf16[192,1024]{1,0:T(8,128)(2,1)}, bf16[192,1024]{1,0:T(8,128)(2,1)}, u32[]{:S(2)}, u32[]{:S(2)}) %collective-permute-start.2) | collective-permute-done | bytes 393248 | tf_op jit(solution)/shard_map/ppermute | solution.py:96
  98.7 8.3 %collective-permute-done.5 = bf16[192,1024]{1,0:T(8,128)(2,1)S(1)} collective-permute-done((bf16[192,1024]{1,0:T(8,128)(2,1)}, bf16[192,1024]{1,0:T(8,128)(2,1)S(1)}, u32[]{:S(2)}, u32[]{:S(2)}) %collective-permute-start.5) | collective-permute-done | bytes 393248 | tf_op jit(solution)/shard_map/ppermute | solution.py:96
  107.0 1.8 constant_dynamic-update-slice_fusion.3
  108.8 1.7 slice.13
  111.0 1.3 concatenate.9.q_ref
  112.3 4.6 %copy.22 = bf16[896,1536]{1,0:T(8,128)(2,1)} copy(bf16[896,1536]{0,1:T(8,128)(2,1)} %bitcast.72) | data formatting | bytes 5505024 | tf_op jit(solution)/shard_map/dot_general | solution.py:171
  116.9 5.6 %convolution_convert_fusion.1 = bf16[1536,1024]{1,0:T(8,128)(2,1)S(1)} fusion(bf16[1536,896]{1,0:T(8,128)(2,1)} %all-gather.2.cloned.1.call-done, bf16[896,1024]{1,0:T(8,128)(2,1)S(1)} %copy-done), kind=kOutput, calls=%fused_computation.1 | convolution fusion | flops 2820145152 | bytes 7733248 | tf_op jit(solution)/shard_map/dot_general | solution.py:164
  122.5 3.6 %convolution_convert_fusion = bf16[1536,1024]{1,0:T(8,128)(2,1)S(1)} fusion(bf16[1536,896]{1,0:T(8,128)(2,1)S(1)} %copy-done.3, bf16[896,1024]{1,0:T(8,128)(2,1)S(1)} %copy-done.13), kind=kOutput, calls=%fused_computation | convolution fusion | flops 2820145152 | bytes 7733248 | tf_op jit(solution)/shard_map/dot_general | solution.py:165
  126.2 17.6 %shard_map.112 = (bf16[768,1024]{1,0:T(8,128)(2,1)S(1)}, bf16[4,12,32,1024]{3,2,1,0:T(8,128)(2,1)S(1)}, bf16[4,12,32,1024]{3,2,1,0:T(8,128)(2,1)S(1)}) custom-call(bf16[768,1024]{1,0:T(8,128)(2,1)S(1)} %copy-done.2, bf16[768,1024]{1,0:T(8,128)(2,1)S(1)} %concatenate.10.g_ref, bf16[4,12,32,1024]{3,2,1,0:T(8,128)(2,1)S(1)} %bitcast.68, ...), custom_call_target="tpu_custom_call" | custom-call | flops 1006632960 | bytes 17301504 | tf_op jit(solution)/shard_map/pallas_call | solution.py:68
  143.7 3.0 %fusion.25 = f32[2,2,2,112,1024]{4,3,2,1,0:T(8,128)S(1)} fusion(bf16[2,2,2,112,1536]{4,3,2,1,0:T(8,128)(2,1)S(1)} %bitcast.73, bf16[1536,1024,1,1,1]{1,0,4,3,2:T(8,128)(2,1)S(1)} %bitcast.71), kind=kOutput, calls=%fused_computation.79 | convolution fusion | flops 2818572288 | bytes 9568256 | tf_op jit(solution)/shard_map/dot_general | solution.py:171
  146.8 1.2 fusion.10
  148.0 1.2 collective-permute-start.12
  149.5 1.9 pad_dynamic-slice_fusion
  151.5 3.0 %fusion.24 = f32[2,2,2,112,1024]{4,3,2,1,0:T(8,128)S(1)} fusion(bf16[2,2,2,112,1536]{4,3,2,1,0:T(8,128)(2,1)S(1)} %bitcast.74, bf16[1536,1024,1,1,1]{1,0,4,3,2:T(8,128)(2,1)S(1)} %bitcast.70), kind=kOutput, calls=%fused_computation.78 | convolution fusion | flops 2818572288 | bytes 9568256 | tf_op jit(solution)/shard_map/dot_general | solution.py:171
  154.6 1.4 collective-permute-start.7
  156.4 1.1 fusion.9
  157.5 1.5 collective-permute-start.8
  159.0 7.6 %collective-permute-done.7 = bf16[192,1024]{1,0:T(8,128)(2,1)S(1)} collective-permute-done((bf16[192,1024]{1,0:T(8,128)(2,1)S(1)}, bf16[192,1024]{1,0:T(8,128)(2,1)S(1)}, u32[]{:S(2)}, u32[]{:S(2)}) %collective-permute-start.7) | collective-permute-done | bytes 393248 | tf_op jit(solution)/shard_map/ppermute | solution.py:96
  166.6 4.2 %collective-permute-done.12 = bf16[2,2,112,1024]{3,2,1,0:T(8,128)(2,1)} collective-permute-done((bf16[2,2,112,1024]{3,2,1,0:T(8,128)(2,1)}, bf16[2,2,112,1024]{3,2,1,0:T(8,128)(2,1)}, u32[]{:S(2)}, u32[]{:S(2)}) %collective-permute-start.12) | collective-permute-done | bytes 917536 | tf_op jit(solution)/shard_map/ppermute | solution.py:121
  170.8 2.3 %bitcast_add_fusion = f32[2,2,112,1024]{3,2,1,0:T(8,128)S(1)} fusion(bf16[2,2,112,1024]{3,2,1,0:T(8,128)(2,1)} %collective-permute-done.12, f32[2,2,2,112,1024]{4,3,2,1,0:T(8,128)} %copy-done.5, s32[]{:T(128)S(6)} %select_n.87), kind=kLoop, calls=%fused_computation.2 | loop fusion | flops 917504 | bytes 4587524 | tf_op jit(solution)/shard_map/add | solution.py:121
  173.3 7.6 %collective-permute-done.9 = bf16[2,2,112,1024]{3,2,1,0:T(8,128)(2,1)} collective-permute-done((bf16[2,2,112,1024]{3,2,1,0:T(8,128)(2,1)}, bf16[2,2,112,1024]{3,2,1,0:T(8,128)(2,1)}, u32[]{:S(2)}, u32[]{:S(2)}) %collective-permute-start.9) | collective-permute-done | bytes 917536 | tf_op jit(solution)/shard_map/ppermute | solution.py:121
  181.0 1.6 bitcast_add_fusion.1
  182.8 11.8 %collective-permute-done.13 = bf16[2,112,1024]{2,1,0:T(8,128)(2,1)S(1)} collective-permute-done((bf16[2,112,1024]{2,1,0:T(8,128)(2,1)S(1)}, bf16[2,112,1024]{2,1,0:T(8,128)(2,1)S(1)}, u32[]{:S(2)}, u32[]{:S(2)}) %collective-permute-start.13) | collective-permute-done | bytes 458784 | tf_op jit(solution)/shard_map/ppermute | solution.py:121
  194.8 1.1 collective-permute-start.14
  195.9 15.9 %collective-permute-done.10 = bf16[2,112,1024]{2,1,0:T(8,128)(2,1)S(1)} collective-permute-done((bf16[2,112,1024]{2,1,0:T(8,128)(2,1)S(1)}, bf16[2,112,1024]{2,1,0:T(8,128)(2,1)S(1)}, u32[]{:S(2)}, u32[]{:S(2)}) %collective-permute-start.10) | collective-permute-done | bytes 458784 | tf_op jit(solution)/shard_map/ppermute | solution.py:121
  212.0 1.1 collective-permute-start.11
  213.0 1.7 collective-permute-done.14
  215.5 2.5 %collective-permute-done.11 = bf16[112,1024]{1,0:T(8,128)(2,1)S(1)} collective-permute-done((bf16[112,1024]{1,0:T(8,128)(2,1)S(1)}, bf16[112,1024]{1,0:T(8,128)(2,1)S(1)}, u32[]{:S(2)}, u32[]{:S(2)}) %collective-permute-start.11) | collective-permute-done | bytes 229408 | tf_op jit(solution)/shard_map/ppermute | solution.py:121
  (81 shorter events, 8.3 us)
Async XLA Ops:
  7.2 109.7 %copy-start = (bf16[896,1024]{1,0:T(8,128)(2,1)S(1)}, bf16[896,1024]{1,0:T(8,128)(2,1)}, u32[]{:S(2)}) copy-start(bf16[896,1024]{1,0:T(8,128)(2,1)} %param.14) | copy-start | bytes 5505028
  7.2 6.0 %copy-start.8 = (bf16[8,32,896]{2,1,0:T(8,128)(2,1)S(1)}, bf16[8,32,896]{2,1,0:T(8,128)(2,1)}, u32[]{:S(2)}) copy-start(bf16[8,32,896]{2,1,0:T(8,128)(2,1)} %param.11) | copy-start | bytes 1376260
  7.2 6.2 %copy-start.12 = (f32[896]{0:T(1024)S(1)}, f32[896]{0:T(1024)}, u32[]{:S(2)}) copy-start(f32[896]{0:T(1024)} %param.12) | copy-start | bytes 10756
  13.6 2.3 %copy-start.11 = (bf16[512,256]{1,0:T(8,128)(2,1)S(1)}, bf16[512,256]{1,0:T(8,128)(2,1)}, u32[]{:S(2)}) copy-start(bf16[512,256]{1,0:T(8,128)(2,1)} %mul.144) | copy-start | bytes 786436
  17.3 30.4 %all-to-all-start = ((bf16[8,64,896]{2,1,0:T(8,128)(2,1)}), bf16[8,64,896]{2,1,0:T(8,128)(2,1)}, u32[]{:S(2)}, u32[]{:S(2)}) async-start(bf16[8,64,896]{2,1,0:T(8,128)(2,1)} %bitcast.2), calls=%async_computation | async-start | bytes 1835008 | tf_op jit(solution)/shard_map/all_to_all | solution.py:148
  24.5 87.7 %all-gather.2.cloned.1.call-start = ((), (), s32[]{:S(2)}) async-start(), calls=%async_computation.1 | async-start | bytes 3440640 | tf_op jit(solution)/shard_map/all_gather | solution.py:153
  50.6 3.9 %copy-start.9 = (bf16[192,4096]{1,0:T(8,128)(2,1)S(1)}, bf16[192,4096]{1,0:T(8,128)(2,1)}, u32[]{:S(2)}) copy-start(bf16[192,4096]{1,0:T(8,128)(2,1)} %param.10) | copy-start | bytes 4718596
  53.2 5.6 %collective-permute-start = (bf16[192,1024]{1,0:T(8,128)(2,1)}, bf16[192,1024]{1,0:T(8,128)(2,1)}, u32[]{:S(2)}, u32[]{:S(2)}) collective-permute-start(bf16[192,1024]{1,0:T(8,128)(2,1)} %get-tuple-element.14), channel_id=1, source_target_pairs={{0,1},{1,0},{2,3},{3,2},{4,5},{5,4},{6,7},{7,6},{8,9},{9,8},{10,11... | collective-permute-start | bytes 1179656 | tf_op jit(solution)/shard_map/ppermute | solution.py:96
  55.7 5.3 %collective-permute-start.3 = (bf16[192,1024]{1,0:T(8,128)(2,1)}, bf16[192,1024]{1,0:T(8,128)(2,1)}, u32[]{:S(2)}, u32[]{:S(2)}) collective-permute-start(bf16[192,1024]{1,0:T(8,128)(2,1)} %get-tuple-element.10), channel_id=1, source_target_pairs={{0,1},{1,0},{2,3},{3,2},{4,5},{5,4},{6,7},{7,6},{8,9},{9,8},{10,11... | collective-permute-start | bytes 1179656 | tf_op jit(solution)/shard_map/ppermute | solution.py:96
  56.2 20.3 %collective-permute-start.1 = (bf16[192,1024]{1,0:T(8,128)(2,1)}, bf16[192,1024]{1,0:T(8,128)(2,1)}, u32[]{:S(2)}, u32[]{:S(2)}) collective-permute-start(bf16[192,1024]{1,0:T(8,128)(2,1)} %get-tuple-element.16), channel_id=1, source_target_pairs={{0,2},{1,3},{2,0},{3,1},{4,6},{5,7},{6,4},{7,5},{8,10},{9,11},{10,... | collective-permute-start | bytes 1179656 | tf_op jit(solution)/shard_map/ppermute | solution.py:96
  57.7 33.5 %collective-permute-start.4 = (bf16[192,1024]{1,0:T(8,128)(2,1)}, bf16[192,1024]{1,0:T(8,128)(2,1)}, u32[]{:S(2)}, u32[]{:S(2)}) collective-permute-start(bf16[192,1024]{1,0:T(8,128)(2,1)} %get-tuple-element.12), channel_id=1, source_target_pairs={{0,2},{1,3},{2,0},{3,1},{4,6},{5,7},{6,4},{7,5},{8,10},{9,11},{10,... | collective-permute-start | bytes 1179656 | tf_op jit(solution)/shard_map/ppermute | solution.py:96
  58.2 40.4 %collective-permute-start.2 = (bf16[192,1024]{1,0:T(8,128)(2,1)}, bf16[192,1024]{1,0:T(8,128)(2,1)}, u32[]{:S(2)}, u32[]{:S(2)}) collective-permute-start(bf16[192,1024]{1,0:T(8,128)(2,1)} %get-tuple-element.13), channel_id=1, source_target_pairs={{0,3},{1,2},{2,1},{3,0},{4,7},{5,6},{6,5},{7,4},{8,11},{9,10},{10,... | collective-permute-start | bytes 1179656 | tf_op jit(solution)/shard_map/ppermute | solution.py:96
  58.8 48.2 %collective-permute-start.5 = (bf16[192,1024]{1,0:T(8,128)(2,1)}, bf16[192,1024]{1,0:T(8,128)(2,1)S(1)}, u32[]{:S(2)}, u32[]{:S(2)}) collective-permute-start(bf16[192,1024]{1,0:T(8,128)(2,1)} %get-tuple-element.9), channel_id=1, source_target_pairs={{0,3},{1,2},{2,1},{3,0},{4,7},{5,6},{6,5},{7,4},{8,11},{9,10},{10,... | collective-permute-start | bytes 1179656 | tf_op jit(solution)/shard_map/ppermute | solution.py:96
  116.9 5.6 %copy-start.3 = (bf16[1536,896]{1,0:T(8,128)(2,1)S(1)}, bf16[1536,896]{1,0:T(8,128)(2,1)}, u32[]{:S(2)}) copy-start(bf16[1536,896]{1,0:T(8,128)(2,1)} %all-gather.2.cloned.1.call-done) | copy-start | bytes 8257540
  116.9 5.6 %copy-start.13 = (bf16[896,1024]{1,0:T(8,128)(2,1)S(1)}, bf16[896,1024]{1,0:T(8,128)(2,1)}, u32[]{:S(2)}) copy-start(bf16[896,1024]{1,0:T(8,128)(2,1)} %param.15) | copy-start | bytes 5505028
  122.5 3.6 %copy-start.2 = (bf16[768,1024]{1,0:T(8,128)(2,1)S(1)}, bf16[768,1024]{1,0:T(8,128)(2,1)}, u32[]{:S(2)}) copy-start(bf16[768,1024]{1,0:T(8,128)(2,1)} %concatenate.9.q_ref) | copy-start | bytes 4718596
  126.2 17.6 %copy-start.4 = (bf16[896,1536]{1,0:T(8,128)(2,1)S(1)}, bf16[896,1536]{1,0:T(8,128)(2,1)}, u32[]{:S(2)}) copy-start(bf16[896,1536]{1,0:T(8,128)(2,1)} %copy.22) | copy-start | bytes 8257540
  146.8 2.6 %copy-start.5 = (f32[2,2,2,112,1024]{4,3,2,1,0:T(8,128)}, f32[2,2,2,112,1024]{4,3,2,1,0:T(8,128)S(1)}, u32[]{:S(2)}) copy-start(f32[2,2,2,112,1024]{4,3,2,1,0:T(8,128)S(1)} %fusion.25) | copy-start | bytes 11010052
  148.0 22.9 %collective-permute-start.12 = (bf16[2,2,112,1024]{3,2,1,0:T(8,128)(2,1)}, bf16[2,2,112,1024]{3,2,1,0:T(8,128)(2,1)}, u32[]{:S(2)}, u32[]{:S(2)}) collective-permute-start(bf16[2,2,112,1024]{3,2,1,0:T(8,128)(2,1)} %fusion.10), channel_id=1, source_target_pairs={{0,4},{4,0},{8,12},{12,8},{16,20},{20,16},{24,28},{28,24},{1,5},{5... | collective-permute-start | bytes 2752520 | tf_op jit(solution)/shard_map/ppermute | solution.py:121
  151.4 7.5 %collective-permute-start.6 = (bf16[192,1024]{1,0:T(8,128)(2,1)S(1)}, bf16[192,1024]{1,0:T(8,128)(2,1)S(1)}, u32[]{:S(2)}, u32[]{:S(2)}) collective-permute-start(bf16[192,1024]{1,0:T(8,128)(2,1)S(1)} %get-tuple-element.18), channel_id=1, source_target_pairs={{0,1},{1,0},{2,3},{3,2},{4,5},{5,4},{6,7},{7,6},{8,9},{9,8},{10,11... | collective-permute-start | bytes 1179656 | tf_op jit(solution)/shard_map/ppermute | solution.py:96
  154.5 1.9 copy-start.6
  154.6 12.0 %collective-permute-start.7 = (bf16[192,1024]{1,0:T(8,128)(2,1)S(1)}, bf16[192,1024]{1,0:T(8,128)(2,1)S(1)}, u32[]{:S(2)}, u32[]{:S(2)}) collective-permute-start(bf16[192,1024]{1,0:T(8,128)(2,1)S(1)} %get-tuple-element.19), channel_id=1, source_target_pairs={{0,2},{1,3},{2,0},{3,1},{4,6},{5,7},{6,4},{7,5},{8,10},{9,11},{10,... | collective-permute-start | bytes 1179656 | tf_op jit(solution)/shard_map/ppermute | solution.py:96
  157.5 23.5 %collective-permute-start.9 = (bf16[2,2,112,1024]{3,2,1,0:T(8,128)(2,1)}, bf16[2,2,112,1024]{3,2,1,0:T(8,128)(2,1)}, u32[]{:S(2)}, u32[]{:S(2)}) collective-permute-start(bf16[2,2,112,1024]{3,2,1,0:T(8,128)(2,1)} %fusion.9), channel_id=1, source_target_pairs={{0,8},{4,12},{8,0},{12,4},{16,24},{20,28},{24,16},{28,20},{1,9},{5... | collective-permute-start | bytes 2752520 | tf_op jit(solution)/shard_map/ppermute | solution.py:121
  157.5 25.2 %collective-permute-start.8 = (bf16[192,1024]{1,0:T(8,128)(2,1)}, bf16[192,1024]{1,0:T(8,128)(2,1)S(1)}, u32[]{:S(2)}, u32[]{:S(2)}) collective-permute-start(bf16[192,1024]{1,0:T(8,128)(2,1)} %get-tuple-element.17), channel_id=1, source_target_pairs={{0,3},{1,2},{2,1},{3,0},{4,7},{5,6},{6,5},{7,4},{8,11},{9,10},{10,... | collective-permute-start | bytes 1179656 | tf_op jit(solution)/shard_map/ppermute | solution.py:96
  170.8 10.1 %copy-start.7 = (f32[2,2,2,112,1024]{4,3,2,1,0:T(8,128)S(1)}, f32[2,2,2,112,1024]{4,3,2,1,0:T(8,128)}, u32[]{:S(2)}) copy-start(f32[2,2,2,112,1024]{4,3,2,1,0:T(8,128)} %copy-done.6) | copy-start | bytes 11010052
  173.2 21.3 %collective-permute-start.13 = (bf16[2,112,1024]{2,1,0:T(8,128)(2,1)S(1)}, bf16[2,112,1024]{2,1,0:T(8,128)(2,1)S(1)}, u32[]{:S(2)}, u32[]{:S(2)}) collective-permute-start(bf16[2,112,1024]{2,1,0:T(8,128)(2,1)S(1)} %fusion.15), channel_id=1, source_target_pairs={{0,8},{4,12},{8,0},{12,4},{16,24},{20,28},{24,16},{28,20},{1,9},{5... | collective-permute-start | bytes 1376264 | tf_op jit(solution)/shard_map/ppermute | solution.py:121
  182.6 29.2 %collective-permute-start.10 = (bf16[2,112,1024]{2,1,0:T(8,128)(2,1)S(1)}, bf16[2,112,1024]{2,1,0:T(8,128)(2,1)S(1)}, u32[]{:S(2)}, u32[]{:S(2)}) collective-permute-start(bf16[2,112,1024]{2,1,0:T(8,128)(2,1)S(1)} %fusion.14), channel_id=1, source_target_pairs={{0,16},{4,20},{8,24},{12,28},{16,0},{20,4},{24,8},{28,12},{1,17},{... | collective-permute-start | bytes 1376264 | tf_op jit(solution)/shard_map/ppermute | solution.py:121
  182.7 29.2 %copy-start.10 = (bf16[192,4096]{1,0:T(8,128)(2,1)}, bf16[192,4096]{1,0:T(8,128)(2,1)S(1)}, u32[]{:S(2)}) copy-start(bf16[192,4096]{1,0:T(8,128)(2,1)S(1)} %constant_dynamic-update-slice_fusion) | copy-start | bytes 4718596
  194.8 19.9 %collective-permute-start.14 = (bf16[112,1024]{1,0:T(8,128)(2,1)S(1)}, bf16[112,1024]{1,0:T(8,128)(2,1)S(1)}, u32[]{:S(2)}, u32[]{:S(2)}) collective-permute-start(bf16[112,1024]{1,0:T(8,128)(2,1)S(1)} %fusion.18), channel_id=1, source_target_pairs={{0,16},{4,20},{8,24},{12,28},{16,0},{20,4},{24,8},{28,12},{1,17},{... | collective-permute-start | bytes 688136 | tf_op jit(solution)/shard_map/ppermute | solution.py:121
  211.8 7.1 %copy-start.1 = (bf16[896,1024]{1,0:T(8,128)(2,1)S(1)}, bf16[896,1024]{1,0:T(8,128)(2,1)}, u32[]{:S(2)}) copy-start(bf16[896,1024]{1,0:T(8,128)(2,1)} %param.14) | copy-start | bytes 5505028
  212.0 6.1 %collective-permute-start.11 = (bf16[112,1024]{1,0:T(8,128)(2,1)S(1)}, bf16[112,1024]{1,0:T(8,128)(2,1)S(1)}, u32[]{:S(2)}, u32[]{:S(2)}) collective-permute-start(bf16[112,1024]{1,0:T(8,128)(2,1)S(1)} %fusion.17), channel_id=1, source_target_pairs={{0,4},{4,0},{8,12},{12,8},{16,20},{20,16},{24,28},{28,24},{1,5},{5... | collective-permute-start | bytes 688136 | tf_op jit(solution)/shard_map/ppermute | solution.py:121
Sparse Core Ops, SparseCore 0:
  50.5 39.9 all-gather.1

commit v3 on v2

--- a/solution.py
+++ b/solution.py
@@ -147,12 +147,14 @@
     outgoing = pick_rows(send, enc, tokens)
     arrived = lax.all_to_all(outgoing, "dp", split_axis=0, concat_axis=0, tiled=True)
 
+    q_rows = exchange(queries, "nbr", 1, 0)
+    arrived, q_rows = lax.optimization_barrier((arrived, q_rows))
+
     place = lax.dynamic_slice_in_dim(owners * CAP + rank, me, 1, 0)[0]
     take = place[:, None] == jnp.arange(dp_count * CAP, dtype=jnp.int32)[None, :]
     picked = pick_rows(take, arrived, tokens)
     flat_enc = lax.all_gather(picked, "nbr", axis=0, tiled=True)
 
-    q_rows = exchange(queries, "nbr", 1, 0)
     g_rows = exchange(cotangent, "nbr", 1, 0)
     seq_len, width = q_rows.shape
     lead = GROUP - 1
@@ -167,14 +169,17 @@
 
     over_first = (((0,), (0,)), ((), ()))
 
-    def weight_grad(grads, turn):
-        product = lax.dot_general(
+    def weight_grad(grads):
+        return lax.dot_general(
             flat_enc, grads.reshape(-1, width), over_first, preferred_element_type=F32
         )
-        return halving(product, "dp", turn)
-
-    grad_v = weight_grad(dv, 0)
-    grad_k = weight_grad(dk, 1)
+
+    grad_v = halving(weight_grad(dv), "dp", 0)
+    product_k = weight_grad(dk)
+    cut = width // HEAD * 3 // 8 * HEAD
+    grad_k = jnp.concatenate(
+        [halving(product_k[:, :cut], "dp", 0), halving(product_k[:, cut:], "dp", 1)], axis=1
+    )
     out = jnp.concatenate([blank, out[: seq_len - lead]], axis=0)
     merged = exchange(out, "nbr", 0, 1)
     return (merged, grad_k, grad_v)

time: 226 us -> 201 us (0.89)
  waiting for transfers between devices: 113 us -> 85.3 us
  starting transfers between devices: 18.2 us -> 25.1 us
  other arithmetic: 10.2 us -> 6.94 us
    all_to_all x1, waiting for transfers between devices: 20.4 us -> 0.01 us  [per_device(): lax.all_to_all(outgoing, 'dp', split_axis=0, concat_axis=0, tiled=True)]
    ppermute x6 -> x9, waiting for transfers between devices: 43.8 us -> 30.6 us  [halving(): current = keep + lax.ppermute(away.astype(BF), axis, pairs).astype(F32)]
    ppermute x6 -> x9, starting transfers between devices: 3.55 us -> 11.2 us  [halving(): current = keep + lax.ppermute(away.astype(BF), axis, pairs).astype(F32)]
    ppermute x9, waiting for transfers between devices: 49 us -> 54.7 us  [exchange(): piece = lax.ppermute(piece, axis, [(i, i ^ d) for i in range(n)])]
    add x6 -> x9, other arithmetic: 5.79 us -> 1.71 us  [halving(): current = keep + lax.ppermute(away.astype(BF), axis, pairs).astype(F32)]
    dynamic_update_slice x8 -> x9, local copies, waits for them, and re-layouts: 7.48 us -> 8.51 us  [exchange(): whole = lax.dynamic_update_slice_in_dim(whole, piece, (me ^ d) * step, join)]
  transfers between devices with their start and end apart: 17 -> 20, of which waited for: 12 -> 12; matrix products, arithmetic and copies ran while one was open for 13% -> 13% of each run, Pallas kernels for 0% -> 0%
where the time goes in v3:
time: 201 us; the launch traced here: 200 us
  waiting for transfers between devices  85.3 us (42%)
  local copies, waits for them, and re-layouts  28.7 us (14%)
  starting transfers between devices  25.1 us (12%)
  matrix products  21.6 us (11%)
  Pallas kernels  17.7 us (9%)
  between operations  14.5 us (7%)
  other arithmetic  6.94 us (3%)
    ppermute x9, waiting for transfers between devices, exchange(): piece = lax.ppermute(piece, axis, [(i, i ^ d) for i in range(n)])  54.7 us
    ppermute x9, waiting for transfers between devices, halving(): current = keep + lax.ppermute(away.astype(BF), axis, pairs).astype(F32)  30.6 us
    pallas_call x1, Pallas kernels, attention(): pl.pallas_call(attention_body, grid=(groups,), in_specs=[row, row, block,...  17.7 us
    ppermute x9, starting transfers between devices, halving(): current = keep + lax.ppermute(away.astype(BF), axis, pairs).astype(F32)  11.2 us
    dynamic_update_slice x9, local copies, waits for them, and re-layouts, exchange(): whole = lax.dynamic_update_slice_in_dim(whole, piece, (me ^ d) * step, join)  8.51 us
    all_to_all x1, starting transfers between devices, per_device(): lax.all_to_all(outgoing, 'dp', split_axis=0, concat_axis=0, tiled=True)  7.4 us
    ppermute x9, starting transfers between devices, exchange(): piece = lax.ppermute(piece, axis, [(i, i ^ d) for i in range(n)])  6.42 us
    dot_general x2, matrix products, weight_grad(): lax.dot_general(flat_enc, grads.reshape(-1, width), over_first, preferred...  6.12 us
  transfers between devices with their start and end apart: 20, of which 12 were waited for; matrix products, arithmetic and copies ran while one was open for 13% of the time, Pallas kernels for 0%

profile of v3, /device:TPU:0, one launch (start us, length us, event | category | flops | bytes accessed | tf_op | source)
XLA Modules:
  0.0 200.0 jit_solution(11932165146659722679)
XLA Ops:
  7.7 1.3 reduce.10
  9.8 1.3 reduce.9
  11.7 1.4 mul.124
  13.6 2.3 %fusion.8 = bf16[256,896]{1,0:T(8,128)(2,1)S(1)} fusion(bf16[8,32,896]{2,1,0:T(8,128)(2,1)S(1)} %copy-done.5, bf16[256,896]{1,0:T(8,128)(2,1)S(1)} %fusion.12, bf16[896,896]{1,0:T(8,128)(2,1)} %param.13), kind=kOutput, calls=%fused_computation.21 | convolution fusion | flops 413564928 | bytes 2981888 | tf_op jit(solution)/shard_map/dot_general | solution.py:19
  15.9 1.4 convolution_convert_fusion.2
  17.3 7.4 %all-to-all-start = ((bf16[8,64,896]{2,1,0:T(8,128)(2,1)}), bf16[8,64,896]{2,1,0:T(8,128)(2,1)}, u32[]{:S(2)}, u32[]{:S(2)}) async-start(bf16[8,64,896]{2,1,0:T(8,128)(2,1)} %bitcast.2), calls=%async_computation | async-start | bytes 1835008 | tf_op jit(solution)/shard_map/all_to_all | solution.py:148
  24.8 1.3 broadcast.73.clone
  26.1 1.2 constant_dynamic-slice_fusion.7
  27.3 1.5 collective-permute-start.1
  29.6 2.4 %mul.150 = bf16[384,512]{1,0:T(8,128)(2,1)} reshape(bf16[12,32,16,32]{3,2,1,0:T(8,128)(2,1)S(1)} %broadcast_multiply_fusion) | data formatting | bytes 786432 | tf_op jit(solution)/shard_map/mul | solution.py:26
  32.0 1.8 constant_dynamic-update-slice_fusion.8
  33.8 5.7 %collective-permute-done.1 = bf16[192,1024]{1,0:T(8,128)(2,1)} collective-permute-done((bf16[192,1024]{1,0:T(8,128)(2,1)}, bf16[192,1024]{1,0:T(8,128)(2,1)}, u32[]{:S(2)}, u32[]{:S(2)}) %collective-permute-start.1) | collective-permute-done | bytes 393248 | tf_op jit(solution)/shard_map/ppermute | solution.py:96
  39.5 1.8 constant_dynamic-update-slice_fusion.7
  41.3 5.9 %collective-permute-done.2 = bf16[192,1024]{1,0:T(8,128)(2,1)} collective-permute-done((bf16[192,1024]{1,0:T(8,128)(2,1)}, bf16[192,1024]{1,0:T(8,128)(2,1)}, u32[]{:S(2)}, u32[]{:S(2)}) %collective-permute-start.2) | collective-permute-done | bytes 393248 | tf_op jit(solution)/shard_map/ppermute | solution.py:96
  47.2 1.8 constant_dynamic-update-slice_fusion.6
  48.9 2.6 %convolution_convert_fusion.3 = bf16[384,896]{1,0:T(8,128)(2,1)} fusion(bf16[384,512]{1,0:T(8,128)(2,1)S(1)} %copy-done.8, bf16[512,896]{1,0:T(8,128)(2,1)} %bitcast.3), kind=kOutput, calls=%fused_computation.6 | convolution fusion | flops 352665600 | bytes 1998848 | tf_op jit(solution)/shard_map/dot_general | solution.py:28
  51.8 2.4 %constant_dynamic-slice_fusion.3 = (bf16[192,1024]{1,0:T(8,128)(2,1)}, bf16[192,1024]{1,0:T(8,128)(2,1)}, bf16[768,1024]{1,0:T(8,128)(2,1)S(1)}, bf16[192,1024]{1,0:T(8,128)(2,1)}) fusion(bf16[192,4096]{1,0:T(8,128)(2,1)} %param.10, s32[]{:T(128)S(6)} %select_n.90, s32[]{:T(128)S(6)} %select_n.86, bf16[768,1024]{1,0:T(8,128)(2,1)S(1)} %broadcast.73.clone.1, ...), kind=kLoop, calls=%fused_computation.69 | loop fusion | bytes 3145748 | tf_op jit(solution)/shard_map/dynamic_slice | solution.py:94
  54.7 1.5 collective-permute-start.4
  56.4 1.0 constant_dynamic-update-slice_fusion.5
  57.4 13.4 %collective-permute-done.4 = bf16[192,1024]{1,0:T(8,128)(2,1)} collective-permute-done((bf16[192,1024]{1,0:T(8,128)(2,1)}, bf16[192,1024]{1,0:T(8,128)(2,1)}, u32[]{:S(2)}, u32[]{:S(2)}) %collective-permute-start.4) | collective-permute-done | bytes 393248 | tf_op jit(solution)/shard_map/ppermute | solution.py:96
  70.8 1.0 constant_dynamic-update-slice_fusion.4
  71.9 14.9 %collective-permute-done.5 = bf16[192,1024]{1,0:T(8,128)(2,1)} collective-permute-done((bf16[192,1024]{1,0:T(8,128)(2,1)}, bf16[192,1024]{1,0:T(8,128)(2,1)}, u32[]{:S(2)}, u32[]{:S(2)}) %collective-permute-start.5) | collective-permute-done | bytes 393248 | tf_op jit(solution)/shard_map/ppermute | solution.py:96
  86.7 1.0 constant_dynamic-update-slice_fusion.3
  88.3 1.7 slice.15
  90.0 1.3 concatenate.12.q_ref
  91.3 4.6 %copy.33 = bf16[896,1536]{1,0:T(8,128)(2,1)} copy(bf16[896,1536]{0,1:T(8,128)(2,1)} %bitcast.90) | data formatting | bytes 5505024 | tf_op jit(solution)/shard_map/dot_general | solution.py:173
  95.9 5.6 %convolution_convert_fusion.1 = bf16[1536,1024]{1,0:T(8,128)(2,1)S(1)} fusion(bf16[1536,896]{1,0:T(8,128)(2,1)} %all-gather.2.cloned.1.call-done, bf16[896,1024]{1,0:T(8,128)(2,1)S(1)} %copy-done), kind=kOutput, calls=%fused_computation.1 | convolution fusion | flops 2820145152 | bytes 7733248 | tf_op jit(solution)/shard_map/dot_general | solution.py:166
  101.5 3.7 %convolution_convert_fusion = bf16[1536,1024]{1,0:T(8,128)(2,1)S(1)} fusion(bf16[1536,896]{1,0:T(8,128)(2,1)S(1)} %copy-done.3, bf16[896,1024]{1,0:T(8,128)(2,1)S(1)} %copy-done.11), kind=kOutput, calls=%fused_computation | convolution fusion | flops 2820145152 | bytes 7733248 | tf_op jit(solution)/shard_map/dot_general | solution.py:167
  105.2 17.7 %shard_map.112 = (bf16[768,1024]{1,0:T(8,128)(2,1)S(1)}, bf16[4,12,32,1024]{3,2,1,0:T(8,128)(2,1)S(1)}, bf16[4,12,32,1024]{3,2,1,0:T(8,128)(2,1)S(1)}) custom-call(bf16[768,1024]{1,0:T(8,128)(2,1)S(1)} %copy-done.2, bf16[768,1024]{1,0:T(8,128)(2,1)S(1)} %concatenate.13.g_ref, bf16[4,12,32,1024]{3,2,1,0:T(8,128)(2,1)S(1)} %bitcast.82, ...), custom_call_target="tpu_custom_call" | custom-call | flops 1006632960 | bytes 17301504 | tf_op jit(solution)/shard_map/pallas_call | solution.py:68
  123.0 3.1 %fusion.27 = f32[896,1024]{1,0:T(8,128)S(1)} fusion(bf16[1536,896]{1,0:T(8,128)(2,1)S(1)} %copy-done.3, bf16[1536,1024]{1,0:T(8,128)(2,1)S(1)} %bitcast.85), kind=kOutput, calls=%fused_computation.90 | convolution fusion | flops 2818572288 | bytes 9568256 | tf_op jit(solution)/shard_map/dot_general | solution.py:173
  126.3 1.9 collective-permute-start.9
  128.2 3.0 %fusion.28 = f32[2,2,2,112,1024]{4,3,2,1,0:T(8,128)S(1)} fusion(bf16[2,2,2,112,1536]{4,3,2,1,0:T(8,128)(2,1)S(1)} %bitcast.91, bf16[1536,1024,1,1,1]{1,0,4,3,2:T(8,128)(2,1)S(1)} %bitcast.84), kind=kOutput, calls=%fused_computation.91 | convolution fusion | flops 2818572288 | bytes 9568256 | tf_op jit(solution)/shard_map/dot_general | solution.py:173
  131.6 1.6 collective-permute-start.15
  133.4 1.2 pad_dynamic-slice_fusion
  134.8 1.5 collective-permute-start.12
  136.3 2.3 %collective-permute-start.7 = (bf16[192,1024]{1,0:T(8,128)(2,1)S(1)}, bf16[192,1024]{1,0:T(8,128)(2,1)S(1)}, u32[]{:S(2)}, u32[]{:S(2)}) collective-permute-start(bf16[192,1024]{1,0:T(8,128)(2,1)S(1)} %get-tuple-element.23), channel_id=1, source_target_pairs={{0,2},{1,3},{2,0},{3,1},{4,6},{5,7},{6,4},{7,5},{8,10},{9,11},{10,... | collective-permute-start | bytes 1179656 | tf_op jit(solution)/shard_map/ppermute | solution.py:96
  138.9 1.8 collective-permute-start.10
  140.7 7.9 %collective-permute-done.7 = bf16[192,1024]{1,0:T(8,128)(2,1)S(1)} collective-permute-done((bf16[192,1024]{1,0:T(8,128)(2,1)S(1)}, bf16[192,1024]{1,0:T(8,128)(2,1)S(1)}, u32[]{:S(2)}, u32[]{:S(2)}) %collective-permute-start.7) | collective-permute-done | bytes 393248 | tf_op jit(solution)/shard_map/ppermute | solution.py:96
  148.6 6.7 %collective-permute-done.8 = bf16[192,1024]{1,0:T(8,128)(2,1)S(1)} collective-permute-done((bf16[192,1024]{1,0:T(8,128)(2,1)S(1)}, bf16[192,1024]{1,0:T(8,128)(2,1)S(1)}, u32[]{:S(2)}, u32[]{:S(2)}) %collective-permute-start.8) | collective-permute-done | bytes 393248 | tf_op jit(solution)/shard_map/ppermute | solution.py:96
  155.5 2.4 %collective-permute-start.11 = (bf16[112,384]{1,0:T(8,128)(2,1)S(1)}, bf16[112,384]{1,0:T(8,128)(2,1)S(1)}, u32[]{:S(2)}, u32[]{:S(2)}) collective-permute-start(bf16[112,384]{1,0:T(8,128)(2,1)S(1)} %fusion.21), channel_id=1, source_target_pairs={{0,16},{4,20},{8,24},{12,28},{16,0},{20,4},{24,8},{28,12},{1,17},{... | collective-permute-start | bytes 258056 | tf_op jit(solution)/shard_map/ppermute | solution.py:121
  158.0 0.9 collective-permute-start.13
  160.1 9.8 %collective-permute-done.11 = bf16[112,384]{1,0:T(8,128)(2,1)S(1)} collective-permute-done((bf16[112,384]{1,0:T(8,128)(2,1)S(1)}, bf16[112,384]{1,0:T(8,128)(2,1)S(1)}, u32[]{:S(2)}, u32[]{:S(2)}) %collective-permute-start.11) | collective-permute-done | bytes 86048 | tf_op jit(solution)/shard_map/ppermute | solution.py:121
  169.9 6.0 %collective-permute-done.13 = bf16[2,112,640]{2,1,0:T(8,128)(2,1)S(1)} collective-permute-done((bf16[2,112,640]{2,1,0:T(8,128)(2,1)S(1)}, bf16[2,112,640]{2,1,0:T(8,128)(2,1)S(1)}, u32[]{:S(2)}, u32[]{:S(2)}) %collective-permute-start.13) | collective-permute-done | bytes 286752 | tf_op jit(solution)/shard_map/ppermute | solution.py:121
  176.5 3.4 %collective-permute-done.16 = bf16[2,112,1024]{2,1,0:T(8,128)(2,1)S(1)} collective-permute-done((bf16[2,112,1024]{2,1,0:T(8,128)(2,1)S(1)}, bf16[2,112,1024]{2,1,0:T(8,128)(2,1)S(1)}, u32[]{:S(2)}, u32[]{:S(2)}) %collective-permute-start.16) | collective-permute-done | bytes 458784 | tf_op jit(solution)/shard_map/ppermute | solution.py:121
  180.3 1.5 collective-permute-done.14
  181.8 0.8 pad_maximum_fusion
  182.6 9.8 %collective-permute-done.17 = bf16[112,1024]{1,0:T(8,128)(2,1)S(1)} collective-permute-done((bf16[112,1024]{1,0:T(8,128)(2,1)S(1)}, bf16[112,1024]{1,0:T(8,128)(2,1)S(1)}, u32[]{:S(2)}, u32[]{:S(2)}) %collective-permute-start.17) | collective-permute-done | bytes 229408 | tf_op jit(solution)/shard_map/ppermute | solution.py:121
  192.4 0.8 bitcast_add_fusion.5
  (93 shorter events, 8.0 us)
Async XLA Ops:
  7.2 88.7 %copy-start = (bf16[896,1024]{1,0:T(8,128)(2,1)S(1)}, bf16[896,1024]{1,0:T(8,128)(2,1)}, u32[]{:S(2)}) copy-start(bf16[896,1024]{1,0:T(8,128)(2,1)} %param.14) | copy-start | bytes 5505028
  7.2 6.0 %copy-start.5 = (bf16[8,32,896]{2,1,0:T(8,128)(2,1)S(1)}, bf16[8,32,896]{2,1,0:T(8,128)(2,1)}, u32[]{:S(2)}) copy-start(bf16[8,32,896]{2,1,0:T(8,128)(2,1)} %param.11) | copy-start | bytes 1376260
  7.2 6.2 %copy-start.10 = (f32[896]{0:T(1024)S(1)}, f32[896]{0:T(1024)}, u32[]{:S(2)}) copy-start(f32[896]{0:T(1024)} %param.12) | copy-start | bytes 10756
  13.6 2.3 %copy-start.9 = (bf16[512,256]{1,0:T(8,128)(2,1)S(1)}, bf16[512,256]{1,0:T(8,128)(2,1)}, u32[]{:S(2)}) copy-start(bf16[512,256]{1,0:T(8,128)(2,1)} %mul.124) | copy-start | bytes 786436
  17.3 8.8 %copy-start.6 = (bf16[192,4096]{1,0:T(8,128)(2,1)S(1)}, bf16[192,4096]{1,0:T(8,128)(2,1)}, u32[]{:S(2)}) copy-start(bf16[192,4096]{1,0:T(8,128)(2,1)} %param.9) | copy-start | bytes 4718596
  17.3 31.6 %all-to-all-start = ((bf16[8,64,896]{2,1,0:T(8,128)(2,1)}), bf16[8,64,896]{2,1,0:T(8,128)(2,1)}, u32[]{:S(2)}, u32[]{:S(2)}) async-start(bf16[8,64,896]{2,1,0:T(8,128)(2,1)} %bitcast.2), calls=%async_computation | async-start | bytes 1835008 | tf_op jit(solution)/shard_map/all_to_all | solution.py:148
  24.7 66.5 %all-gather.2.cloned.1.call-start = ((), (), s32[]{:S(2)}) async-start(), calls=%async_computation.1 | async-start | bytes 3440640 | tf_op jit(solution)/shard_map/all_gather | solution.py:156
  27.3 4.7 %collective-permute-start = (bf16[192,1024]{1,0:T(8,128)(2,1)}, bf16[192,1024]{1,0:T(8,128)(2,1)}, u32[]{:S(2)}, u32[]{:S(2)}) collective-permute-start(bf16[192,1024]{1,0:T(8,128)(2,1)} %get-tuple-element.18), channel_id=1, source_target_pairs={{0,1},{1,0},{2,3},{3,2},{4,5},{5,4},{6,7},{7,6},{8,9},{9,8},{10,11... | collective-permute-start | bytes 1179656 | tf_op jit(solution)/shard_map/ppermute | solution.py:96
  27.3 12.2 %collective-permute-start.1 = (bf16[192,1024]{1,0:T(8,128)(2,1)}, bf16[192,1024]{1,0:T(8,128)(2,1)}, u32[]{:S(2)}, u32[]{:S(2)}) collective-permute-start(bf16[192,1024]{1,0:T(8,128)(2,1)} %get-tuple-element.20), channel_id=1, source_target_pairs={{0,2},{1,3},{2,0},{3,1},{4,6},{5,7},{6,4},{7,5},{8,10},{9,11},{10,... | collective-permute-start | bytes 1179656 | tf_op jit(solution)/shard_map/ppermute | solution.py:96
  28.8 18.4 %collective-permute-start.2 = (bf16[192,1024]{1,0:T(8,128)(2,1)}, bf16[192,1024]{1,0:T(8,128)(2,1)}, u32[]{:S(2)}, u32[]{:S(2)}) collective-permute-start(bf16[192,1024]{1,0:T(8,128)(2,1)} %get-tuple-element.17), channel_id=1, source_target_pairs={{0,3},{1,2},{2,1},{3,0},{4,7},{5,6},{6,5},{7,4},{8,11},{9,10},{10,... | collective-permute-start | bytes 1179656 | tf_op jit(solution)/shard_map/ppermute | solution.py:96
  32.0 17.0 %copy-start.8 = (bf16[384,512]{1,0:T(8,128)(2,1)S(1)}, bf16[384,512]{1,0:T(8,128)(2,1)}, u32[]{:S(2)}) copy-start(bf16[384,512]{1,0:T(8,128)(2,1)} %mul.150) | copy-start | bytes 1179652
  54.2 2.2 %collective-permute-start.3 = (bf16[192,1024]{1,0:T(8,128)(2,1)}, bf16[192,1024]{1,0:T(8,128)(2,1)}, u32[]{:S(2)}, u32[]{:S(2)}) collective-permute-start(bf16[192,1024]{1,0:T(8,128)(2,1)} %get-tuple-element.14), channel_id=1, source_target_pairs={{0,1},{1,0},{2,3},{3,2},{4,5},{5,4},{6,7},{7,6},{8,9},{9,8},{10,11... | collective-permute-start | bytes 1179656 | tf_op jit(solution)/shard_map/ppermute | solution.py:96
  54.7 16.2 %collective-permute-start.4 = (bf16[192,1024]{1,0:T(8,128)(2,1)}, bf16[192,1024]{1,0:T(8,128)(2,1)}, u32[]{:S(2)}, u32[]{:S(2)}) collective-permute-start(bf16[192,1024]{1,0:T(8,128)(2,1)} %get-tuple-element.16), channel_id=1, source_target_pairs={{0,2},{1,3},{2,0},{3,1},{4,6},{5,7},{6,4},{7,5},{8,10},{9,11},{10,... | collective-permute-start | bytes 1179656 | tf_op jit(solution)/shard_map/ppermute | solution.py:96
  56.2 30.6 %collective-permute-start.5 = (bf16[192,1024]{1,0:T(8,128)(2,1)}, bf16[192,1024]{1,0:T(8,128)(2,1)}, u32[]{:S(2)}, u32[]{:S(2)}) collective-permute-start(bf16[192,1024]{1,0:T(8,128)(2,1)} %get-tuple-element.13), channel_id=1, source_target_pairs={{0,3},{1,2},{2,1},{3,0},{4,7},{5,6},{6,5},{7,4},{8,11},{9,10},{10,... | collective-permute-start | bytes 1179656 | tf_op jit(solution)/shard_map/ppermute | solution.py:96
  95.9 5.6 %copy-start.3 = (bf16[1536,896]{1,0:T(8,128)(2,1)S(1)}, bf16[1536,896]{1,0:T(8,128)(2,1)}, u32[]{:S(2)}) copy-start(bf16[1536,896]{1,0:T(8,128)(2,1)} %all-gather.2.cloned.1.call-done) | copy-start | bytes 8257540
  95.9 5.6 %copy-start.11 = (bf16[896,1024]{1,0:T(8,128)(2,1)S(1)}, bf16[896,1024]{1,0:T(8,128)(2,1)}, u32[]{:S(2)}) copy-start(bf16[896,1024]{1,0:T(8,128)(2,1)} %param.15) | copy-start | bytes 5505028
  101.5 3.7 %copy-start.2 = (bf16[768,1024]{1,0:T(8,128)(2,1)S(1)}, bf16[768,1024]{1,0:T(8,128)(2,1)}, u32[]{:S(2)}) copy-start(bf16[768,1024]{1,0:T(8,128)(2,1)} %concatenate.12.q_ref) | copy-start | bytes 4718596
  126.1 2.1 %copy-start.4 = (bf16[896,1536]{1,0:T(8,128)(2,1)S(1)}, bf16[896,1536]{1,0:T(8,128)(2,1)}, u32[]{:S(2)}) copy-start(bf16[896,1536]{1,0:T(8,128)(2,1)} %copy.33) | copy-start | bytes 8257540
  126.3 12.3 %collective-permute-start.9 = (bf16[2,2,112,384]{3,2,0,1:T(8,128)(2,1)S(1)}, bf16[2,2,112,384]{3,2,0,1:T(8,128)(2,1)S(1)}, u32[]{:S(2)}, u32[]{:S(2)}) collective-permute-start(bf16[2,2,112,384]{3,2,0,1:T(8,128)(2,1)S(1)} %fusion.16), channel_id=1, source_target_pairs={{0,4},{4,0},{8,12},{12,8},{16,20},{20,16},{24,28},{28,24},{1,5},{5... | collective-permute-start | bytes 1032200 | tf_op jit(solution)/shard_map/ppermute | solution.py:121
  131.6 27.3 %collective-permute-start.15 = (bf16[2,2,112,1024]{3,2,1,0:T(8,128)(2,1)S(1)}, bf16[2,2,112,1024]{3,2,1,0:T(8,128)(2,1)S(1)}, u32[]{:S(2)}, u32[]{:S(2)}) collective-permute-start(bf16[2,2,112,1024]{3,2,1,0:T(8,128)(2,1)S(1)} %fusion.9), channel_id=1, source_target_pairs={{0,4},{4,0},{8,12},{12,8},{16,20},{20,16},{24,28},{28,24},{1,5},{5... | collective-permute-start | bytes 2752520 | tf_op jit(solution)/shard_map/ppermute | solution.py:121
  134.6 4.3 %collective-permute-start.6 = (bf16[192,1024]{1,0:T(8,128)(2,1)S(1)}, bf16[192,1024]{1,0:T(8,128)(2,1)S(1)}, u32[]{:S(2)}, u32[]{:S(2)}) collective-permute-start(bf16[192,1024]{1,0:T(8,128)(2,1)S(1)} %get-tuple-element.22), channel_id=1, source_target_pairs={{0,1},{1,0},{2,3},{3,2},{4,5},{5,4},{6,7},{7,6},{8,9},{9,8},{10,11... | collective-permute-start | bytes 1179656 | tf_op jit(solution)/shard_map/ppermute | solution.py:96
  134.8 23.1 %collective-permute-start.12 = (bf16[2,2,112,640]{3,2,1,0:T(8,128)(2,1)S(1)}, bf16[2,2,112,640]{3,2,1,0:T(8,128)(2,1)S(1)}, u32[]{:S(2)}, u32[]{:S(2)}) collective-permute-start(bf16[2,2,112,640]{3,2,1,0:T(8,128)(2,1)S(1)} %fusion.13), channel_id=1, source_target_pairs={{0,8},{4,12},{8,0},{12,4},{16,24},{20,28},{24,16},{28,20},{1,9},{5... | collective-permute-start | bytes 1720328 | tf_op jit(solution)/shard_map/ppermute | solution.py:121
  136.3 12.3 %collective-permute-start.7 = (bf16[192,1024]{1,0:T(8,128)(2,1)S(1)}, bf16[192,1024]{1,0:T(8,128)(2,1)S(1)}, u32[]{:S(2)}, u32[]{:S(2)}) collective-permute-start(bf16[192,1024]{1,0:T(8,128)(2,1)S(1)} %get-tuple-element.23), channel_id=1, source_target_pairs={{0,2},{1,3},{2,0},{3,1},{4,6},{5,7},{6,4},{7,5},{8,10},{9,11},{10,... | collective-permute-start | bytes 1179656 | tf_op jit(solution)/shard_map/ppermute | solution.py:96
  138.6 16.7 %collective-permute-start.8 = (bf16[192,1024]{1,0:T(8,128)(2,1)S(1)}, bf16[192,1024]{1,0:T(8,128)(2,1)S(1)}, u32[]{:S(2)}, u32[]{:S(2)}) collective-permute-start(bf16[192,1024]{1,0:T(8,128)(2,1)S(1)} %get-tuple-element.21), channel_id=1, source_target_pairs={{0,3},{1,2},{2,1},{3,0},{4,7},{5,6},{6,5},{7,4},{8,11},{9,10},{10,... | collective-permute-start | bytes 1179656 | tf_op jit(solution)/shard_map/ppermute | solution.py:96
  138.9 16.5 %collective-permute-start.10 = (bf16[2,112,384]{2,1,0:T(8,128)(2,1)S(1)}, bf16[2,112,384]{2,1,0:T(8,128)(2,1)S(1)}, u32[]{:S(2)}, u32[]{:S(2)}) collective-permute-start(bf16[2,112,384]{2,1,0:T(8,128)(2,1)S(1)} %fusion.19), channel_id=1, source_target_pairs={{0,8},{4,12},{8,0},{12,4},{16,24},{20,28},{24,16},{28,20},{1,9},{5... | collective-permute-start | bytes 516104 | tf_op jit(solution)/shard_map/ppermute | solution.py:121
  155.4 2.6 %copy-start.7 = (bf16[192,4096]{1,0:T(8,128)(2,1)}, bf16[192,4096]{1,0:T(8,128)(2,1)S(1)}, u32[]{:S(2)}) copy-start(bf16[192,4096]{1,0:T(8,128)(2,1)S(1)} %constant_dynamic-update-slice_fusion) | copy-start | bytes 4718596
  155.5 14.4 %collective-permute-start.11 = (bf16[112,384]{1,0:T(8,128)(2,1)S(1)}, bf16[112,384]{1,0:T(8,128)(2,1)S(1)}, u32[]{:S(2)}, u32[]{:S(2)}) collective-permute-start(bf16[112,384]{1,0:T(8,128)(2,1)S(1)} %fusion.21), channel_id=1, source_target_pairs={{0,16},{4,20},{8,24},{12,28},{16,0},{20,4},{24,8},{28,12},{1,17},{... | collective-permute-start | bytes 258056 | tf_op jit(solution)/shard_map/ppermute | solution.py:121
  158.0 17.9 %collective-permute-start.13 = (bf16[2,112,640]{2,1,0:T(8,128)(2,1)S(1)}, bf16[2,112,640]{2,1,0:T(8,128)(2,1)S(1)}, u32[]{:S(2)}, u32[]{:S(2)}) collective-permute-start(bf16[2,112,640]{2,1,0:T(8,128)(2,1)S(1)} %fusion.17), channel_id=1, source_target_pairs={{0,16},{4,20},{8,24},{12,28},{16,0},{20,4},{24,8},{28,12},{1,17},{... | collective-permute-start | bytes 860168 | tf_op jit(solution)/shard_map/ppermute | solution.py:121
  159.4 20.6 %collective-permute-start.16 = (bf16[2,112,1024]{2,1,0:T(8,128)(2,1)S(1)}, bf16[2,112,1024]{2,1,0:T(8,128)(2,1)S(1)}, u32[]{:S(2)}, u32[]{:S(2)}) collective-permute-start(bf16[2,112,1024]{2,1,0:T(8,128)(2,1)S(1)} %fusion.14), channel_id=1, source_target_pairs={{0,8},{4,12},{8,0},{12,4},{16,24},{20,28},{24,16},{28,20},{1,9},{5... | collective-permute-start | bytes 1376264 | tf_op jit(solution)/shard_map/ppermute | solution.py:121
  176.0 5.7 %collective-permute-start.14 = (bf16[112,640]{1,0:T(8,128)(2,1)S(1)}, bf16[112,640]{1,0:T(8,128)(2,1)S(1)}, u32[]{:S(2)}, u32[]{:S(2)}) collective-permute-start(bf16[112,640]{1,0:T(8,128)(2,1)S(1)} %fusion.20), channel_id=1, source_target_pairs={{0,4},{4,0},{8,12},{12,8},{16,20},{20,16},{24,28},{28,24},{1,5},{5... | collective-permute-start | bytes 430088 | tf_op jit(solution)/shard_map/ppermute | solution.py:121
  180.0 13.2 %copy-start.1 = (bf16[896,1024]{1,0:T(8,128)(2,1)S(1)}, bf16[896,1024]{1,0:T(8,128)(2,1)}, u32[]{:S(2)}) copy-start(bf16[896,1024]{1,0:T(8,128)(2,1)} %param.14) | copy-start | bytes 5505028
  180.2 12.2 %collective-permute-start.17 = (bf16[112,1024]{1,0:T(8,128)(2,1)S(1)}, bf16[112,1024]{1,0:T(8,128)(2,1)S(1)}, u32[]{:S(2)}, u32[]{:S(2)}) collective-permute-start(bf16[112,1024]{1,0:T(8,128)(2,1)S(1)} %fusion.18), channel_id=1, source_target_pairs={{0,16},{4,20},{8,24},{12,28},{16,0},{20,4},{24,8},{28,12},{1,17},{... | collective-permute-start | bytes 688136 | tf_op jit(solution)/shard_map/ppermute | solution.py:121
Sparse Core Ops, SparseCore 0:
  51.7 38.9 all-gather.1

commit v4 on v3

--- a/solution.py
+++ b/solution.py
@@ -148,14 +148,14 @@
     arrived = lax.all_to_all(outgoing, "dp", split_axis=0, concat_axis=0, tiled=True)
 
     q_rows = exchange(queries, "nbr", 1, 0)
-    arrived, q_rows = lax.optimization_barrier((arrived, q_rows))
+    g_rows = exchange(cotangent, "nbr", 1, 0)
+    arrived, q_rows, g_rows = lax.optimization_barrier((arrived, q_rows, g_rows))
 
     place = lax.dynamic_slice_in_dim(owners * CAP + rank, me, 1, 0)[0]
     take = place[:, None] == jnp.arange(dp_count * CAP, dtype=jnp.int32)[None, :]
     picked = pick_rows(take, arrived, tokens)
     flat_enc = lax.all_gather(picked, "nbr", axis=0, tiled=True)
 
-    g_rows = exchange(cotangent, "nbr", 1, 0)
     seq_len, width = q_rows.shape
     lead = GROUP - 1
     blank = jnp.zeros((lead, width), BF)

time: 201 us -> 203 us (level)
  waiting for transfers between devices: 85.3 us -> 90 us
  starting transfers between devices: 25.1 us -> 22.7 us
    all_gather x1, waiting for transfers between devices: 0.01 us -> 24.2 us  [per_device(): flat_enc = lax.all_gather(picked, 'nbr', axis=0, tiled=True)]
    ppermute x9, waiting for transfers between devices: 54.7 us -> 34.7 us  [exchange(): piece = lax.ppermute(piece, axis, [(i, i ^ d) for i in range(n)])]
  transfers between devices with their start and end apart: 20 -> 20, of which waited for: 12 -> 11; matrix products, arithmetic and copies ran while one was open for 13% -> 13% of each run, Pallas kernels for 0% -> 0%
where the time goes in v4:
time: 203 us; the launch traced here: 202 us
  waiting for transfers between devices  90 us (44%)
  local copies, waits for them, and re-layouts  28.7 us (14%)
  starting transfers between devices  22.7 us (11%)
  matrix products  21.6 us (11%)
  Pallas kernels  17.7 us (9%)
  between operations  14.6 us (7%)
  other arithmetic  6.91 us (3%)
    ppermute x9, waiting for transfers between devices, exchange(): piece = lax.ppermute(piece, axis, [(i, i ^ d) for i in range(n)])  34.7 us
    ppermute x9, waiting for transfers between devices, halving(): current = keep + lax.ppermute(away.astype(BF), axis, pairs).astype(F32)  31.2 us
    all_gather x1, waiting for transfers between devices, per_device(): flat_enc = lax.all_gather(picked, 'nbr', axis=0, tiled=True)  24.2 us
    pallas_call x1, Pallas kernels, attention(): pl.pallas_call(attention_body, grid=(groups,), in_specs=[row, row, block,...  17.7 us
    ppermute x9, starting transfers between devices, halving(): current = keep + lax.ppermute(away.astype(BF), axis, pairs).astype(F32)  10.6 us
    dynamic_update_slice x9, local copies, waits for them, and re-layouts, exchange(): whole = lax.dynamic_update_slice_in_dim(whole, piece, (me ^ d) * step, join)  9.74 us
    all_to_all x1, starting transfers between devices, per_device(): lax.all_to_all(outgoing, 'dp', split_axis=0, concat_axis=0, tiled=True)  7.41 us
    dot_general x2, matrix products, weight_grad(): lax.dot_general(flat_enc, grads.reshape(-1, width), over_first, preferred...  6.12 us
  transfers between devices with their start and end apart: 20, of which 11 were waited for; matrix products, arithmetic and copies ran while one was open for 13% of the time, Pallas kernels for 0%

profile of v4, /device:TPU:0, one launch (start us, length us, event | category | flops | bytes accessed | tf_op | source)
XLA Modules:
  0.0 202.3 jit_solution(6782295858922411192)
XLA Ops:
  7.7 1.3 reduce.10
  9.8 1.3 reduce.9
  11.7 1.4 mul.124
  13.6 2.2 %fusion.8 = bf16[256,896]{1,0:T(8,128)(2,1)S(1)} fusion(bf16[8,32,896]{2,1,0:T(8,128)(2,1)S(1)} %copy-done.8, bf16[256,896]{1,0:T(8,128)(2,1)S(1)} %fusion.12, bf16[896,896]{1,0:T(8,128)(2,1)} %param.13), kind=kOutput, calls=%fused_computation.21 | convolution fusion | flops 413564928 | bytes 2981888 | tf_op jit(solution)/shard_map/dot_general | solution.py:19
  15.9 1.4 convolution_convert_fusion.2
  17.3 7.4 %all-to-all-start = ((bf16[8,64,896]{2,1,0:T(8,128)(2,1)}), bf16[8,64,896]{2,1,0:T(8,128)(2,1)}, u32[]{:S(2)}, u32[]{:S(2)}) async-start(bf16[8,64,896]{2,1,0:T(8,128)(2,1)} %bitcast.2), calls=%async_computation | async-start | bytes 1835008 | tf_op jit(solution)/shard_map/all_to_all | solution.py:148
  25.0 1.1 constant_dynamic-slice_fusion.3
  26.1 1.6 collective-permute-start.4
  28.2 1.1 constant_dynamic-slice_fusion.7
  29.3 1.1 copy-done.5
  30.8 1.5 collective-permute-start.1
  32.7 2.3 %mul.150 = bf16[384,512]{1,0:T(8,128)(2,1)} reshape(bf16[12,32,16,32]{3,2,1,0:T(8,128)(2,1)S(1)} %broadcast_multiply_fusion) | data formatting | bytes 786432 | tf_op jit(solution)/shard_map/mul | solution.py:26
  35.0 1.8 constant_dynamic-update-slice_fusion.5
  36.8 1.8 constant_dynamic-update-slice_fusion.8
  38.5 1.8 constant_dynamic-update-slice_fusion.4
  40.4 14.9 %collective-permute-done.1 = bf16[192,1024]{1,0:T(8,128)(2,1)} collective-permute-done((bf16[192,1024]{1,0:T(8,128)(2,1)}, bf16[192,1024]{1,0:T(8,128)(2,1)}, u32[]{:S(2)}, u32[]{:S(2)}) %collective-permute-start.1) | collective-permute-done | bytes 393248 | tf_op jit(solution)/shard_map/ppermute | solution.py:96
  55.3 1.8 constant_dynamic-update-slice_fusion.7
  57.0 1.8 constant_dynamic-update-slice_fusion.3
  58.8 3.9 %collective-permute-done.2 = bf16[192,1024]{1,0:T(8,128)(2,1)S(1)} collective-permute-done((bf16[192,1024]{1,0:T(8,128)(2,1)}, bf16[192,1024]{1,0:T(8,128)(2,1)S(1)}, u32[]{:S(2)}, u32[]{:S(2)}) %collective-permute-start.2) | collective-permute-done | bytes 393248 | tf_op jit(solution)/shard_map/ppermute | solution.py:96
  62.7 0.8 constant_dynamic-update-slice_fusion.6
  63.5 2.6 %convolution_convert_fusion.3 = bf16[384,896]{1,0:T(8,128)(2,1)} fusion(bf16[384,512]{1,0:T(8,128)(2,1)S(1)} %copy-done.12, bf16[512,896]{1,0:T(8,128)(2,1)} %bitcast.3), kind=kOutput, calls=%fused_computation.6 | convolution fusion | flops 352665600 | bytes 1998848 | tf_op jit(solution)/shard_map/dot_general | solution.py:28
  66.1 1.8 slice.15
  68.5 1.3 concatenate.13.g_ref
  69.7 24.2 %all-gather.2.cloned.1.call-done = bf16[1536,896]{1,0:T(8,128)(2,1)} async-done(((bf16[384,896]{1,0:T(8,128)(2,1)}), bf16[1536,896]{1,0:T(8,128)(2,1)}) %all-gather.2.cloned.1.call-update) | async-done | bytes 2752528 | tf_op jit(solution)/shard_map/all_gather | solution.py:157
  93.9 4.7 %copy.33 = bf16[896,1536]{1,0:T(8,128)(2,1)} copy(bf16[896,1536]{0,1:T(8,128)(2,1)} %bitcast.90) | data formatting | bytes 5505024 | tf_op jit(solution)/shard_map/dot_general | solution.py:173
  98.6 5.6 %convolution_convert_fusion.1 = bf16[1536,1024]{1,0:T(8,128)(2,1)S(1)} fusion(bf16[1536,896]{1,0:T(8,128)(2,1)} %all-gather.2.cloned.1.call-done, bf16[896,1024]{1,0:T(8,128)(2,1)S(1)} %copy-done), kind=kOutput, calls=%fused_computation.1 | convolution fusion | flops 2820145152 | bytes 7733248 | tf_op jit(solution)/shard_map/dot_general | solution.py:166
  104.2 3.7 %convolution_convert_fusion = bf16[1536,1024]{1,0:T(8,128)(2,1)S(1)} fusion(bf16[1536,896]{1,0:T(8,128)(2,1)S(1)} %copy-done.6, bf16[896,1024]{1,0:T(8,128)(2,1)S(1)} %copy-done.15), kind=kOutput, calls=%fused_computation | convolution fusion | flops 2820145152 | bytes 7733248 | tf_op jit(solution)/shard_map/dot_general | solution.py:167
  107.9 17.7 %shard_map.112 = (bf16[768,1024]{1,0:T(8,128)(2,1)S(1)}, bf16[4,12,32,1024]{3,2,1,0:T(8,128)(2,1)S(1)}, bf16[4,12,32,1024]{3,2,1,0:T(8,128)(2,1)S(1)}) custom-call(bf16[768,1024]{1,0:T(8,128)(2,1)S(1)} %concatenate.12.q_ref, bf16[768,1024]{1,0:T(8,128)(2,1)S(1)} %copy-done.2, bf16[4,12,32,1024]{3,2,1,0:T(8,128)(2,1)S(1)} %bitcast.82, ...), custom_call_target="tpu_custom_call" | custom-call | flops 1006632960 | bytes 17301504 | tf_op jit(solution)/shard_map/pallas_call | solution.py:68
  125.6 3.1 %fusion.27 = f32[896,1024]{1,0:T(8,128)S(1)} fusion(bf16[1536,896]{1,0:T(8,128)(2,1)S(1)} %copy-done.6, bf16[1536,1024]{1,0:T(8,128)(2,1)S(1)} %bitcast.85), kind=kOutput, calls=%fused_computation.90 | convolution fusion | flops 2818572288 | bytes 9568256 | tf_op jit(solution)/shard_map/dot_general | solution.py:173
  128.9 1.5 collective-permute-start.9
  130.5 3.0 %fusion.28 = f32[2,2,2,112,1024]{4,3,2,1,0:T(8,128)S(1)} fusion(bf16[2,2,2,112,1536]{4,3,2,1,0:T(8,128)(2,1)S(1)} %bitcast.91, bf16[1536,1024,1,1,1]{1,0,4,3,2:T(8,128)(2,1)S(1)} %bitcast.84), kind=kOutput, calls=%fused_computation.91 | convolution fusion | flops 2818572288 | bytes 9568256 | tf_op jit(solution)/shard_map/dot_general | solution.py:173
  133.9 1.5 collective-permute-start.15
  135.7 1.2 pad_dynamic-slice_fusion
  137.0 1.6 collective-permute-start.12
  139.2 0.7 collective-permute-done.9
  140.3 1.3 collective-permute-start.10
  141.6 8.9 %collective-permute-done.7 = bf16[192,1024]{1,0:T(8,128)(2,1)S(1)} collective-permute-done((bf16[192,1024]{1,0:T(8,128)(2,1)S(1)}, bf16[192,1024]{1,0:T(8,128)(2,1)S(1)}, u32[]{:S(2)}, u32[]{:S(2)}) %collective-permute-start.7) | collective-permute-done | bytes 393248 | tf_op jit(solution)/shard_map/ppermute | solution.py:96
  150.6 6.9 %collective-permute-done.8 = bf16[192,1024]{1,0:T(8,128)(2,1)S(1)} collective-permute-done((bf16[192,1024]{1,0:T(8,128)(2,1)S(1)}, bf16[192,1024]{1,0:T(8,128)(2,1)S(1)}, u32[]{:S(2)}, u32[]{:S(2)}) %collective-permute-start.8) | collective-permute-done | bytes 393248 | tf_op jit(solution)/shard_map/ppermute | solution.py:96
  157.6 2.5 %collective-permute-start.11 = (bf16[112,384]{1,0:T(8,128)(2,1)S(1)}, bf16[112,384]{1,0:T(8,128)(2,1)S(1)}, u32[]{:S(2)}, u32[]{:S(2)}) collective-permute-start(bf16[112,384]{1,0:T(8,128)(2,1)S(1)} %fusion.21), channel_id=1, source_target_pairs={{0,16},{4,20},{8,24},{12,28},{16,0},{20,4},{24,8},{28,12},{1,17},{... | collective-permute-start | bytes 258056 | tf_op jit(solution)/shard_map/ppermute | solution.py:121
  160.3 0.9 collective-permute-start.13
  162.3 9.7 %collective-permute-done.11 = bf16[112,384]{1,0:T(8,128)(2,1)S(1)} collective-permute-done((bf16[112,384]{1,0:T(8,128)(2,1)S(1)}, bf16[112,384]{1,0:T(8,128)(2,1)S(1)}, u32[]{:S(2)}, u32[]{:S(2)}) %collective-permute-start.11) | collective-permute-done | bytes 86048 | tf_op jit(solution)/shard_map/ppermute | solution.py:121
  172.0 6.1 %collective-permute-done.13 = bf16[2,112,640]{2,1,0:T(8,128)(2,1)S(1)} collective-permute-done((bf16[2,112,640]{2,1,0:T(8,128)(2,1)S(1)}, bf16[2,112,640]{2,1,0:T(8,128)(2,1)S(1)}, u32[]{:S(2)}, u32[]{:S(2)}) %collective-permute-start.13) | collective-permute-done | bytes 286752 | tf_op jit(solution)/shard_map/ppermute | solution.py:121
  178.2 0.6 collective-permute-start.14
  178.8 3.4 %collective-permute-done.16 = bf16[2,112,1024]{2,1,0:T(8,128)(2,1)S(1)} collective-permute-done((bf16[2,112,1024]{2,1,0:T(8,128)(2,1)S(1)}, bf16[2,112,1024]{2,1,0:T(8,128)(2,1)S(1)}, u32[]{:S(2)}, u32[]{:S(2)}) %collective-permute-start.16) | collective-permute-done | bytes 458784 | tf_op jit(solution)/shard_map/ppermute | solution.py:121
  182.5 1.5 collective-permute-done.14
  184.0 0.8 pad_maximum_fusion
  184.8 9.8 %collective-permute-done.17 = bf16[112,1024]{1,0:T(8,128)(2,1)S(1)} collective-permute-done((bf16[112,1024]{1,0:T(8,128)(2,1)S(1)}, bf16[112,1024]{1,0:T(8,128)(2,1)S(1)}, u32[]{:S(2)}, u32[]{:S(2)}) %collective-permute-start.17) | collective-permute-done | bytes 229408 | tf_op jit(solution)/shard_map/ppermute | solution.py:121
  194.6 0.8 bitcast_add_fusion.5
  (101 shorter events, 8.0 us)
Async XLA Ops:
  7.2 91.4 %copy-start = (bf16[896,1024]{1,0:T(8,128)(2,1)S(1)}, bf16[896,1024]{1,0:T(8,128)(2,1)}, u32[]{:S(2)}) copy-start(bf16[896,1024]{1,0:T(8,128)(2,1)} %param.14) | copy-start | bytes 5505028
  7.2 6.0 %copy-start.8 = (bf16[8,32,896]{2,1,0:T(8,128)(2,1)S(1)}, bf16[8,32,896]{2,1,0:T(8,128)(2,1)}, u32[]{:S(2)}) copy-start(bf16[8,32,896]{2,1,0:T(8,128)(2,1)} %param.11) | copy-start | bytes 1376260
  7.2 6.2 %copy-start.14 = (f32[896]{0:T(1024)S(1)}, f32[896]{0:T(1024)}, u32[]{:S(2)}) copy-start(f32[896]{0:T(1024)} %param.12) | copy-start | bytes 10756
  13.6 2.3 %copy-start.13 = (bf16[512,256]{1,0:T(8,128)(2,1)S(1)}, bf16[512,256]{1,0:T(8,128)(2,1)}, u32[]{:S(2)}) copy-start(bf16[512,256]{1,0:T(8,128)(2,1)} %mul.124) | copy-start | bytes 786436
  17.3 7.7 %copy-start.9 = (bf16[192,4096]{1,0:T(8,128)(2,1)S(1)}, bf16[192,4096]{1,0:T(8,128)(2,1)}, u32[]{:S(2)}) copy-start(bf16[192,4096]{1,0:T(8,128)(2,1)} %param.10) | copy-start | bytes 4718596
  17.3 46.1 %all-to-all-start = ((bf16[8,64,896]{2,1,0:T(8,128)(2,1)}), bf16[8,64,896]{2,1,0:T(8,128)(2,1)}, u32[]{:S(2)}, u32[]{:S(2)}) async-start(bf16[8,64,896]{2,1,0:T(8,128)(2,1)} %bitcast.2), calls=%async_computation | async-start | bytes 1835008 | tf_op jit(solution)/shard_map/all_to_all | solution.py:148
  24.7 69.2 %all-gather.2.cloned.1.call-start = ((), (), s32[]{:S(2)}) async-start(), calls=%async_computation.1 | async-start | bytes 3440640 | tf_op jit(solution)/shard_map/all_gather | solution.py:157
  26.1 3.2 %copy-start.3 = (bf16[768,1024]{1,0:T(8,128)(2,1)}, bf16[768,1024]{1,0:T(8,128)(2,1)S(1)}, u32[]{:S(2)}) copy-start(bf16[768,1024]{1,0:T(8,128)(2,1)S(1)} %get-tuple-element.17) | copy-start | bytes 4718596
  26.1 2.1 %copy-start.10 = (bf16[192,4096]{1,0:T(8,128)(2,1)S(1)}, bf16[192,4096]{1,0:T(8,128)(2,1)}, u32[]{:S(2)}) copy-start(bf16[192,4096]{1,0:T(8,128)(2,1)} %param.9) | copy-start | bytes 4718596
  26.1 8.9 %collective-permute-start.3 = (bf16[192,1024]{1,0:T(8,128)(2,1)}, bf16[192,1024]{1,0:T(8,128)(2,1)}, u32[]{:S(2)}, u32[]{:S(2)}) collective-permute-start(bf16[192,1024]{1,0:T(8,128)(2,1)} %get-tuple-element.16), channel_id=1, source_target_pairs={{0,1},{1,0},{2,3},{3,2},{4,5},{5,4},{6,7},{7,6},{8,9},{9,8},{10,11... | collective-permute-start | bytes 1179656 | tf_op jit(solution)/shard_map/ppermute | solution.py:96
  26.1 12.4 %collective-permute-start.4 = (bf16[192,1024]{1,0:T(8,128)(2,1)}, bf16[192,1024]{1,0:T(8,128)(2,1)}, u32[]{:S(2)}, u32[]{:S(2)}) collective-permute-start(bf16[192,1024]{1,0:T(8,128)(2,1)} %get-tuple-element.18), channel_id=1, source_target_pairs={{0,2},{1,3},{2,0},{3,1},{4,6},{5,7},{6,4},{7,5},{8,10},{9,11},{10,... | collective-permute-start | bytes 1179656 | tf_op jit(solution)/shard_map/ppermute | solution.py:96
  27.7 29.4 %collective-permute-start.5 = (bf16[192,1024]{1,0:T(8,128)(2,1)}, bf16[192,1024]{1,0:T(8,128)(2,1)}, u32[]{:S(2)}, u32[]{:S(2)}) collective-permute-start(bf16[192,1024]{1,0:T(8,128)(2,1)} %get-tuple-element.15), channel_id=1, source_target_pairs={{0,3},{1,2},{2,1},{3,0},{4,7},{5,6},{6,5},{7,4},{8,11},{9,10},{10,... | collective-permute-start | bytes 1179656 | tf_op jit(solution)/shard_map/ppermute | solution.py:96
  29.3 1.1 copy-start.5
  30.4 6.3 %collective-permute-start = (bf16[192,1024]{1,0:T(8,128)(2,1)}, bf16[192,1024]{1,0:T(8,128)(2,1)}, u32[]{:S(2)}, u32[]{:S(2)}) collective-permute-start(bf16[192,1024]{1,0:T(8,128)(2,1)} %get-tuple-element.20), channel_id=1, source_target_pairs={{0,1},{1,0},{2,3},{3,2},{4,5},{5,4},{6,7},{7,6},{8,9},{9,8},{10,11... | collective-permute-start | bytes 1179656 | tf_op jit(solution)/shard_map/ppermute | solution.py:96
  30.8 24.5 %collective-permute-start.1 = (bf16[192,1024]{1,0:T(8,128)(2,1)}, bf16[192,1024]{1,0:T(8,128)(2,1)}, u32[]{:S(2)}, u32[]{:S(2)}) collective-permute-start(bf16[192,1024]{1,0:T(8,128)(2,1)} %get-tuple-element.22), channel_id=1, source_target_pairs={{0,2},{1,3},{2,0},{3,1},{4,6},{5,7},{6,4},{7,5},{8,10},{9,11},{10,... | collective-permute-start | bytes 1179656 | tf_op jit(solution)/shard_map/ppermute | solution.py:96
  35.0 27.7 %collective-permute-start.2 = (bf16[192,1024]{1,0:T(8,128)(2,1)}, bf16[192,1024]{1,0:T(8,128)(2,1)S(1)}, u32[]{:S(2)}, u32[]{:S(2)}) collective-permute-start(bf16[192,1024]{1,0:T(8,128)(2,1)} %get-tuple-element.19), channel_id=1, source_target_pairs={{0,3},{1,2},{2,1},{3,0},{4,7},{5,6},{6,5},{7,4},{8,11},{9,10},{10,... | collective-permute-start | bytes 1179656 | tf_op jit(solution)/shard_map/ppermute | solution.py:96
  38.5 24.9 %copy-start.12 = (bf16[384,512]{1,0:T(8,128)(2,1)S(1)}, bf16[384,512]{1,0:T(8,128)(2,1)}, u32[]{:S(2)}) copy-start(bf16[384,512]{1,0:T(8,128)(2,1)} %mul.150) | copy-start | bytes 1179652
  66.1 1.9 copy-start.4
  98.6 5.6 %copy-start.6 = (bf16[1536,896]{1,0:T(8,128)(2,1)S(1)}, bf16[1536,896]{1,0:T(8,128)(2,1)}, u32[]{:S(2)}) copy-start(bf16[1536,896]{1,0:T(8,128)(2,1)} %all-gather.2.cloned.1.call-done) | copy-start | bytes 8257540
  98.6 5.6 %copy-start.15 = (bf16[896,1024]{1,0:T(8,128)(2,1)S(1)}, bf16[896,1024]{1,0:T(8,128)(2,1)}, u32[]{:S(2)}) copy-start(bf16[896,1024]{1,0:T(8,128)(2,1)} %param.15) | copy-start | bytes 5505028
  104.2 3.7 %copy-start.2 = (bf16[768,1024]{1,0:T(8,128)(2,1)S(1)}, bf16[768,1024]{1,0:T(8,128)(2,1)}, u32[]{:S(2)}) copy-start(bf16[768,1024]{1,0:T(8,128)(2,1)} %concatenate.13.g_ref) | copy-start | bytes 4718596
  128.7 1.8 copy-start.7
  128.9 11.0 %collective-permute-start.9 = (bf16[2,2,112,384]{3,2,0,1:T(8,128)(2,1)S(1)}, bf16[2,2,112,384]{3,2,0,1:T(8,128)(2,1)S(1)}, u32[]{:S(2)}, u32[]{:S(2)}) collective-permute-start(bf16[2,2,112,384]{3,2,0,1:T(8,128)(2,1)S(1)} %fusion.16), channel_id=1, source_target_pairs={{0,4},{4,0},{8,12},{12,8},{16,20},{20,16},{24,28},{28,24},{1,5},{5... | collective-permute-start | bytes 1032200 | tf_op jit(solution)/shard_map/ppermute | solution.py:121
  133.9 27.3 %collective-permute-start.15 = (bf16[2,2,112,1024]{3,2,1,0:T(8,128)(2,1)S(1)}, bf16[2,2,112,1024]{3,2,1,0:T(8,128)(2,1)S(1)}, u32[]{:S(2)}, u32[]{:S(2)}) collective-permute-start(bf16[2,2,112,1024]{3,2,1,0:T(8,128)(2,1)S(1)} %fusion.9), channel_id=1, source_target_pairs={{0,4},{4,0},{8,12},{12,8},{16,20},{20,16},{24,28},{28,24},{1,5},{5... | collective-permute-start | bytes 2752520 | tf_op jit(solution)/shard_map/ppermute | solution.py:121
  136.9 3.4 %collective-permute-start.6 = (bf16[192,1024]{1,0:T(8,128)(2,1)S(1)}, bf16[192,1024]{1,0:T(8,128)(2,1)S(1)}, u32[]{:S(2)}, u32[]{:S(2)}) collective-permute-start(bf16[192,1024]{1,0:T(8,128)(2,1)S(1)} %get-tuple-element.24), channel_id=1, source_target_pairs={{0,1},{1,0},{2,3},{3,2},{4,5},{5,4},{6,7},{7,6},{8,9},{9,8},{10,11... | collective-permute-start | bytes 1179656 | tf_op jit(solution)/shard_map/ppermute | solution.py:96
  137.0 23.1 %collective-permute-start.12 = (bf16[2,2,112,640]{3,2,1,0:T(8,128)(2,1)S(1)}, bf16[2,2,112,640]{3,2,1,0:T(8,128)(2,1)S(1)}, u32[]{:S(2)}, u32[]{:S(2)}) collective-permute-start(bf16[2,2,112,640]{3,2,1,0:T(8,128)(2,1)S(1)} %fusion.13), channel_id=1, source_target_pairs={{0,8},{4,12},{8,0},{12,4},{16,24},{20,28},{24,16},{28,20},{1,9},{5... | collective-permute-start | bytes 1720328 | tf_op jit(solution)/shard_map/ppermute | solution.py:121
  138.6 12.0 %collective-permute-start.7 = (bf16[192,1024]{1,0:T(8,128)(2,1)S(1)}, bf16[192,1024]{1,0:T(8,128)(2,1)S(1)}, u32[]{:S(2)}, u32[]{:S(2)}) collective-permute-start(bf16[192,1024]{1,0:T(8,128)(2,1)S(1)} %get-tuple-element.25), channel_id=1, source_target_pairs={{0,2},{1,3},{2,0},{3,1},{4,6},{5,7},{6,4},{7,5},{8,10},{9,11},{10,... | collective-permute-start | bytes 1179656 | tf_op jit(solution)/shard_map/ppermute | solution.py:96
  139.9 17.6 %collective-permute-start.8 = (bf16[192,1024]{1,0:T(8,128)(2,1)S(1)}, bf16[192,1024]{1,0:T(8,128)(2,1)S(1)}, u32[]{:S(2)}, u32[]{:S(2)}) collective-permute-start(bf16[192,1024]{1,0:T(8,128)(2,1)S(1)} %get-tuple-element.23), channel_id=1, source_target_pairs={{0,3},{1,2},{2,1},{3,0},{4,7},{5,6},{6,5},{7,4},{8,11},{9,10},{10,... | collective-permute-start | bytes 1179656 | tf_op jit(solution)/shard_map/ppermute | solution.py:96
  140.3 17.3 %collective-permute-start.10 = (bf16[2,112,384]{2,1,0:T(8,128)(2,1)S(1)}, bf16[2,112,384]{2,1,0:T(8,128)(2,1)S(1)}, u32[]{:S(2)}, u32[]{:S(2)}) collective-permute-start(bf16[2,112,384]{2,1,0:T(8,128)(2,1)S(1)} %fusion.19), channel_id=1, source_target_pairs={{0,8},{4,12},{8,0},{12,4},{16,24},{20,28},{24,16},{28,20},{1,9},{5... | collective-permute-start | bytes 516104 | tf_op jit(solution)/shard_map/ppermute | solution.py:121
  157.6 2.7 %copy-start.11 = (bf16[192,4096]{1,0:T(8,128)(2,1)}, bf16[192,4096]{1,0:T(8,128)(2,1)S(1)}, u32[]{:S(2)}) copy-start(bf16[192,4096]{1,0:T(8,128)(2,1)S(1)} %constant_dynamic-update-slice_fusion) | copy-start | bytes 4718596
  157.6 14.3 %collective-permute-start.11 = (bf16[112,384]{1,0:T(8,128)(2,1)S(1)}, bf16[112,384]{1,0:T(8,128)(2,1)S(1)}, u32[]{:S(2)}, u32[]{:S(2)}) collective-permute-start(bf16[112,384]{1,0:T(8,128)(2,1)S(1)} %fusion.21), channel_id=1, source_target_pairs={{0,16},{4,20},{8,24},{12,28},{16,0},{20,4},{24,8},{28,12},{1,17},{... | collective-permute-start | bytes 258056 | tf_op jit(solution)/shard_map/ppermute | solution.py:121
  160.3 17.8 %collective-permute-start.13 = (bf16[2,112,640]{2,1,0:T(8,128)(2,1)S(1)}, bf16[2,112,640]{2,1,0:T(8,128)(2,1)S(1)}, u32[]{:S(2)}, u32[]{:S(2)}) collective-permute-start(bf16[2,112,640]{2,1,0:T(8,128)(2,1)S(1)} %fusion.17), channel_id=1, source_target_pairs={{0,16},{4,20},{8,24},{12,28},{16,0},{20,4},{24,8},{28,12},{1,17},{... | collective-permute-start | bytes 860168 | tf_op jit(solution)/shard_map/ppermute | solution.py:121
  161.7 20.5 %collective-permute-start.16 = (bf16[2,112,1024]{2,1,0:T(8,128)(2,1)S(1)}, bf16[2,112,1024]{2,1,0:T(8,128)(2,1)S(1)}, u32[]{:S(2)}, u32[]{:S(2)}) collective-permute-start(bf16[2,112,1024]{2,1,0:T(8,128)(2,1)S(1)} %fusion.14), channel_id=1, source_target_pairs={{0,8},{4,12},{8,0},{12,4},{16,24},{20,28},{24,16},{28,20},{1,9},{5... | collective-permute-start | bytes 1376264 | tf_op jit(solution)/shard_map/ppermute | solution.py:121
  178.2 5.8 %collective-permute-start.14 = (bf16[112,640]{1,0:T(8,128)(2,1)S(1)}, bf16[112,640]{1,0:T(8,128)(2,1)S(1)}, u32[]{:S(2)}, u32[]{:S(2)}) collective-permute-start(bf16[112,640]{1,0:T(8,128)(2,1)S(1)} %fusion.20), channel_id=1, source_target_pairs={{0,4},{4,0},{8,12},{12,8},{16,20},{20,16},{24,28},{28,24},{1,5},{5... | collective-permute-start | bytes 430088 | tf_op jit(solution)/shard_map/ppermute | solution.py:121
  182.2 13.2 %copy-start.1 = (bf16[896,1024]{1,0:T(8,128)(2,1)S(1)}, bf16[896,1024]{1,0:T(8,128)(2,1)}, u32[]{:S(2)}) copy-start(bf16[896,1024]{1,0:T(8,128)(2,1)} %param.14) | copy-start | bytes 5505028
  182.4 12.2 %collective-permute-start.17 = (bf16[112,1024]{1,0:T(8,128)(2,1)S(1)}, bf16[112,1024]{1,0:T(8,128)(2,1)S(1)}, u32[]{:S(2)}, u32[]{:S(2)}) collective-permute-start(bf16[112,1024]{1,0:T(8,128)(2,1)S(1)} %fusion.18), channel_id=1, source_target_pairs={{0,16},{4,20},{8,24},{12,28},{16,0},{20,4},{24,8},{28,12},{1,17},{... | collective-permute-start | bytes 688136 | tf_op jit(solution)/shard_map/ppermute | solution.py:121
Sparse Core Ops, SparseCore 0:
  66.2 27.6 all-gather.1

commit v5 on v3

--- a/solution.py
+++ b/solution.py
@@ -175,11 +175,7 @@
         )
 
     grad_v = halving(weight_grad(dv), "dp", 0)
-    product_k = weight_grad(dk)
-    cut = width // HEAD * 3 // 8 * HEAD
-    grad_k = jnp.concatenate(
-        [halving(product_k[:, :cut], "dp", 0), halving(product_k[:, cut:], "dp", 1)], axis=1
-    )
+    grad_k = halving(weight_grad(dk), "dp", 1)
     out = jnp.concatenate([blank, out[: seq_len - lead]], axis=0)
     merged = exchange(out, "nbr", 0, 1)
     return (merged, grad_k, grad_v)

time: 201 us -> 206 us (1.025)
  other arithmetic: 6.94 us -> 10.2 us
  waiting for transfers between devices: 85.3 us -> 87.7 us
  local copies, waits for them, and re-layouts: 28.7 us -> 31.1 us
  starting transfers between devices: 25.1 us -> 22.8 us
    ppermute x9 -> x6, waiting for transfers between devices: 30.6 us -> 41.3 us  [halving(): current = keep + lax.ppermute(away.astype(BF), axis, pairs).astype(F32)]
    ppermute x9, waiting for transfers between devices: 54.7 us -> 46.4 us  [exchange(): piece = lax.ppermute(piece, axis, [(i, i ^ d) for i in range(n)])]
    add x9 -> x6, other arithmetic: 1.71 us -> 5.79 us  [halving(): current = keep + lax.ppermute(away.astype(BF), axis, pairs).astype(F32)]
    ppermute x9 -> x6, starting transfers between devices: 11.2 us -> 7.98 us  [halving(): current = keep + lax.ppermute(away.astype(BF), axis, pairs).astype(F32)]
  transfers between devices with their start and end apart: 20 -> 17, of which waited for: 12 -> 12; matrix products, arithmetic and copies ran while one was open for 13% -> 15% of each run, Pallas kernels for 0% -> 0%
where the time goes in v5:
time: 206 us; the launch traced here: 205 us
  waiting for transfers between devices  87.7 us (43%)
  local copies, waits for them, and re-layouts  31.1 us (15%)
  starting transfers between devices  22.8 us (11%)
  matrix products  21.5 us (10%)
  Pallas kernels  17.6 us (9%)
  between operations  14.5 us (7%)
  other arithmetic  10.2 us (5%)
    ppermute x9, waiting for transfers between devices, exchange(): piece = lax.ppermute(piece, axis, [(i, i ^ d) for i in range(n)])  46.4 us
    ppermute x6, waiting for transfers between devices, halving(): current = keep + lax.ppermute(away.astype(BF), axis, pairs).astype(F32)  41.3 us
    pallas_call x1, Pallas kernels, attention(): pl.pallas_call(attention_body, grid=(groups,), in_specs=[row, row, block,...  17.6 us
    dynamic_update_slice x9, local copies, waits for them, and re-layouts, exchange(): whole = lax.dynamic_update_slice_in_dim(whole, piece, (me ^ d) * step, join)  8.52 us
    ppermute x6, starting transfers between devices, halving(): current = keep + lax.ppermute(away.astype(BF), axis, pairs).astype(F32)  7.98 us
    all_to_all x1, starting transfers between devices, per_device(): lax.all_to_all(outgoing, 'dp', split_axis=0, concat_axis=0, tiled=True)  7.4 us
    ppermute x9, starting transfers between devices, exchange(): piece = lax.ppermute(piece, axis, [(i, i ^ d) for i in range(n)])  7.39 us
    dot_general x2, matrix products, weight_grad(): lax.dot_general(flat_enc, grads.reshape(-1, width), over_first, preferred...  6 us
  transfers between devices with their start and end apart: 17, of which 12 were waited for; matrix products, arithmetic and copies ran while one was open for 15% of the time, Pallas kernels for 0%

profile of v5, /device:TPU:0, one launch (start us, length us, event | category | flops | bytes accessed | tf_op | source)
XLA Modules:
  0.0 205.3 jit_solution(48976753630907380)
XLA Ops:
  7.7 1.3 reduce.10
  9.8 1.3 reduce.9
  11.7 1.4 mul.124
  13.6 2.3 %fusion.8 = bf16[256,896]{1,0:T(8,128)(2,1)S(1)} fusion(bf16[8,32,896]{2,1,0:T(8,128)(2,1)S(1)} %copy-done.8, bf16[256,896]{1,0:T(8,128)(2,1)S(1)} %fusion.13, bf16[896,896]{1,0:T(8,128)(2,1)} %param.13), kind=kOutput, calls=%fused_computation.21 | convolution fusion | flops 413564928 | bytes 2981888 | tf_op jit(solution)/shard_map/dot_general | solution.py:19
  15.9 1.4 convolution_convert_fusion.2
  17.3 7.4 %all-to-all-start = ((bf16[8,64,896]{2,1,0:T(8,128)(2,1)}), bf16[8,64,896]{2,1,0:T(8,128)(2,1)}, u32[]{:S(2)}, u32[]{:S(2)}) async-start(bf16[8,64,896]{2,1,0:T(8,128)(2,1)} %bitcast.2), calls=%async_computation | async-start | bytes 1835008 | tf_op jit(solution)/shard_map/all_to_all | solution.py:148
  24.8 1.3 broadcast.73.clone
  26.1 1.2 constant_dynamic-slice_fusion.5
  27.3 1.5 collective-permute-start.1
  29.6 2.4 %mul.150 = bf16[384,512]{1,0:T(8,128)(2,1)} reshape(bf16[12,32,16,32]{3,2,1,0:T(8,128)(2,1)S(1)} %broadcast_multiply_fusion) | data formatting | bytes 786432 | tf_op jit(solution)/shard_map/mul | solution.py:26
  32.0 1.8 constant_dynamic-update-slice_fusion.8
  33.8 5.7 %collective-permute-done.1 = bf16[192,1024]{1,0:T(8,128)(2,1)} collective-permute-done((bf16[192,1024]{1,0:T(8,128)(2,1)}, bf16[192,1024]{1,0:T(8,128)(2,1)}, u32[]{:S(2)}, u32[]{:S(2)}) %collective-permute-start.1) | collective-permute-done | bytes 393248 | tf_op jit(solution)/shard_map/ppermute | solution.py:96
  39.5 1.8 constant_dynamic-update-slice_fusion.7
  41.3 5.9 %collective-permute-done.2 = bf16[192,1024]{1,0:T(8,128)(2,1)} collective-permute-done((bf16[192,1024]{1,0:T(8,128)(2,1)}, bf16[192,1024]{1,0:T(8,128)(2,1)}, u32[]{:S(2)}, u32[]{:S(2)}) %collective-permute-start.2) | collective-permute-done | bytes 393248 | tf_op jit(solution)/shard_map/ppermute | solution.py:96
  47.2 1.8 constant_dynamic-update-slice_fusion.6
  48.9 2.6 %convolution_convert_fusion.3 = bf16[384,896]{1,0:T(8,128)(2,1)} fusion(bf16[384,512]{1,0:T(8,128)(2,1)S(1)} %copy-done.11, bf16[512,896]{1,0:T(8,128)(2,1)} %bitcast.3), kind=kOutput, calls=%fused_computation.8 | convolution fusion | flops 352665600 | bytes 1998848 | tf_op jit(solution)/shard_map/dot_general | solution.py:28
  51.8 2.4 %constant_dynamic-slice_fusion.1 = (bf16[192,1024]{1,0:T(8,128)(2,1)}, bf16[192,1024]{1,0:T(8,128)(2,1)}, bf16[768,1024]{1,0:T(8,128)(2,1)S(1)}, bf16[192,1024]{1,0:T(8,128)(2,1)}) fusion(bf16[192,4096]{1,0:T(8,128)(2,1)} %param.10, s32[]{:T(128)S(6)} %select_n.80, s32[]{:T(128)S(6)} %select_n.76, bf16[768,1024]{1,0:T(8,128)(2,1)S(1)} %broadcast.73.clone.1, ...), kind=kLoop, calls=%fused_computation.57 | loop fusion | bytes 3145748 | tf_op jit(solution)/shard_map/dynamic_slice | solution.py:94
  54.7 1.5 collective-permute-start.4
  56.4 1.0 constant_dynamic-update-slice_fusion.5
  57.4 13.4 %collective-permute-done.4 = bf16[192,1024]{1,0:T(8,128)(2,1)} collective-permute-done((bf16[192,1024]{1,0:T(8,128)(2,1)}, bf16[192,1024]{1,0:T(8,128)(2,1)}, u32[]{:S(2)}, u32[]{:S(2)}) %collective-permute-start.4) | collective-permute-done | bytes 393248 | tf_op jit(solution)/shard_map/ppermute | solution.py:96
  70.8 1.0 constant_dynamic-update-slice_fusion.4
  71.9 14.9 %collective-permute-done.5 = bf16[192,1024]{1,0:T(8,128)(2,1)} collective-permute-done((bf16[192,1024]{1,0:T(8,128)(2,1)}, bf16[192,1024]{1,0:T(8,128)(2,1)}, u32[]{:S(2)}, u32[]{:S(2)}) %collective-permute-start.5) | collective-permute-done | bytes 393248 | tf_op jit(solution)/shard_map/ppermute | solution.py:96
  88.3 1.7 slice.9
  90.0 1.3 concatenate.9.q_ref
  91.3 4.6 %copy.22 = bf16[896,1536]{1,0:T(8,128)(2,1)} copy(bf16[896,1536]{0,1:T(8,128)(2,1)} %bitcast.72) | data formatting | bytes 5505024 | tf_op jit(solution)/shard_map/dot_general | solution.py:173
  95.9 5.6 %convolution_convert_fusion.1 = bf16[1536,1024]{1,0:T(8,128)(2,1)S(1)} fusion(bf16[1536,896]{1,0:T(8,128)(2,1)} %all-gather.2.cloned.1.call-done, bf16[896,1024]{1,0:T(8,128)(2,1)S(1)} %copy-done), kind=kOutput, calls=%fused_computation.1 | convolution fusion | flops 2820145152 | bytes 7733248 | tf_op jit(solution)/shard_map/dot_general | solution.py:166
  101.5 3.6 %convolution_convert_fusion = bf16[1536,1024]{1,0:T(8,128)(2,1)S(1)} fusion(bf16[1536,896]{1,0:T(8,128)(2,1)S(1)} %copy-done.3, bf16[896,1024]{1,0:T(8,128)(2,1)S(1)} %copy-done.14), kind=kOutput, calls=%fused_computation | convolution fusion | flops 2820145152 | bytes 7733248 | tf_op jit(solution)/shard_map/dot_general | solution.py:167
  105.2 17.6 %shard_map.112 = (bf16[768,1024]{1,0:T(8,128)(2,1)S(1)}, bf16[4,12,32,1024]{3,2,1,0:T(8,128)(2,1)S(1)}, bf16[4,12,32,1024]{3,2,1,0:T(8,128)(2,1)S(1)}) custom-call(bf16[768,1024]{1,0:T(8,128)(2,1)S(1)} %copy-done.2, bf16[768,1024]{1,0:T(8,128)(2,1)S(1)} %concatenate.10.g_ref, bf16[4,12,32,1024]{3,2,1,0:T(8,128)(2,1)S(1)} %bitcast.68, ...), custom_call_target="tpu_custom_call" | custom-call | flops 1006632960 | bytes 17301504 | tf_op jit(solution)/shard_map/pallas_call | solution.py:68
  122.7 3.0 %fusion.25 = f32[2,2,2,112,1024]{4,3,2,1,0:T(8,128)S(1)} fusion(bf16[2,2,2,112,1536]{4,3,2,1,0:T(8,128)(2,1)S(1)} %bitcast.73, bf16[1536,1024,1,1,1]{1,0,4,3,2:T(8,128)(2,1)S(1)} %bitcast.71), kind=kOutput, calls=%fused_computation.79 | convolution fusion | flops 2818572288 | bytes 9568256 | tf_op jit(solution)/shard_map/dot_general | solution.py:173
  125.8 1.2 fusion.10
  127.0 1.9 collective-permute-start.12
  129.1 1.9 pad_dynamic-slice_fusion
  131.0 3.0 %fusion.24 = f32[2,2,2,112,1024]{4,3,2,1,0:T(8,128)S(1)} fusion(bf16[2,2,2,112,1536]{4,3,2,1,0:T(8,128)(2,1)S(1)} %bitcast.74, bf16[1536,1024,1,1,1]{1,0,4,3,2:T(8,128)(2,1)S(1)} %bitcast.70), kind=kOutput, calls=%fused_computation.78 | convolution fusion | flops 2818572288 | bytes 9568256 | tf_op jit(solution)/shard_map/dot_general | solution.py:173
  134.0 2.4 %collective-permute-start.7 = (bf16[192,1024]{1,0:T(8,128)(2,1)S(1)}, bf16[192,1024]{1,0:T(8,128)(2,1)S(1)}, u32[]{:S(2)}, u32[]{:S(2)}) collective-permute-start(bf16[192,1024]{1,0:T(8,128)(2,1)S(1)} %get-tuple-element.23), channel_id=1, source_target_pairs={{0,2},{1,3},{2,0},{3,1},{4,6},{5,7},{6,4},{7,5},{8,10},{9,11},{10,... | collective-permute-start | bytes 1179656 | tf_op jit(solution)/shard_map/ppermute | solution.py:96
  136.4 1.1 fusion.9
  137.5 1.4 collective-permute-start.9
  138.9 1.1 collective-permute-start.8
  140.1 6.3 %collective-permute-done.7 = bf16[192,1024]{1,0:T(8,128)(2,1)S(1)} collective-permute-done((bf16[192,1024]{1,0:T(8,128)(2,1)S(1)}, bf16[192,1024]{1,0:T(8,128)(2,1)S(1)}, u32[]{:S(2)}, u32[]{:S(2)}) %collective-permute-start.7) | collective-permute-done | bytes 393248 | tf_op jit(solution)/shard_map/ppermute | solution.py:96
  146.4 3.4 %collective-permute-done.12 = bf16[2,2,112,1024]{3,2,1,0:T(8,128)(2,1)} collective-permute-done((bf16[2,2,112,1024]{3,2,1,0:T(8,128)(2,1)}, bf16[2,2,112,1024]{3,2,1,0:T(8,128)(2,1)}, u32[]{:S(2)}, u32[]{:S(2)}) %collective-permute-start.12) | collective-permute-done | bytes 917536 | tf_op jit(solution)/shard_map/ppermute | solution.py:121
  149.8 2.3 %bitcast_add_fusion = f32[2,2,112,1024]{3,2,1,0:T(8,128)S(1)} fusion(bf16[2,2,112,1024]{3,2,1,0:T(8,128)(2,1)} %collective-permute-done.12, f32[2,2,2,112,1024]{4,3,2,1,0:T(8,128)} %copy-done.5, s32[]{:T(128)S(6)} %select_n.87), kind=kLoop, calls=%fused_computation.2 | loop fusion | flops 917504 | bytes 4587524 | tf_op jit(solution)/shard_map/add | solution.py:121
  152.2 1.8 collective-permute-start.13
  154.0 7.0 %collective-permute-done.9 = bf16[2,2,112,1024]{3,2,1,0:T(8,128)(2,1)} collective-permute-done((bf16[2,2,112,1024]{3,2,1,0:T(8,128)(2,1)}, bf16[2,2,112,1024]{3,2,1,0:T(8,128)(2,1)}, u32[]{:S(2)}, u32[]{:S(2)}) %collective-permute-start.9) | collective-permute-done | bytes 917536 | tf_op jit(solution)/shard_map/ppermute | solution.py:121
  161.0 1.6 bitcast_add_fusion.1
  162.7 2.4 %collective-permute-start.10 = (bf16[2,112,1024]{2,1,0:T(8,128)(2,1)S(1)}, bf16[2,112,1024]{2,1,0:T(8,128)(2,1)S(1)}, u32[]{:S(2)}, u32[]{:S(2)}) collective-permute-start(bf16[2,112,1024]{2,1,0:T(8,128)(2,1)S(1)} %fusion.14), channel_id=1, source_target_pairs={{0,16},{4,20},{8,24},{12,28},{16,0},{20,4},{24,8},{28,12},{1,17},{... | collective-permute-start | bytes 1376264 | tf_op jit(solution)/shard_map/ppermute | solution.py:121
  165.1 11.8 %collective-permute-done.13 = bf16[2,112,1024]{2,1,0:T(8,128)(2,1)S(1)} collective-permute-done((bf16[2,112,1024]{2,1,0:T(8,128)(2,1)S(1)}, bf16[2,112,1024]{2,1,0:T(8,128)(2,1)S(1)}, u32[]{:S(2)}, u32[]{:S(2)}) %collective-permute-start.13) | collective-permute-done | bytes 458784 | tf_op jit(solution)/shard_map/ppermute | solution.py:121
  177.3 14.1 %collective-permute-done.10 = bf16[2,112,1024]{2,1,0:T(8,128)(2,1)S(1)} collective-permute-done((bf16[2,112,1024]{2,1,0:T(8,128)(2,1)S(1)}, bf16[2,112,1024]{2,1,0:T(8,128)(2,1)S(1)}, u32[]{:S(2)}, u32[]{:S(2)}) %collective-permute-start.10) | collective-permute-done | bytes 458784 | tf_op jit(solution)/shard_map/ppermute | solution.py:121
  192.0 1.8 collective-permute-done.14
  194.7 3.0 %collective-permute-done.11 = bf16[112,1024]{1,0:T(8,128)(2,1)S(1)} collective-permute-done((bf16[112,1024]{1,0:T(8,128)(2,1)S(1)}, bf16[112,1024]{1,0:T(8,128)(2,1)S(1)}, u32[]{:S(2)}, u32[]{:S(2)}) %collective-permute-start.11) | collective-permute-done | bytes 229408 | tf_op jit(solution)/shard_map/ppermute | solution.py:121
  (84 shorter events, 8.5 us)
Async XLA Ops:
  7.2 88.7 %copy-start = (bf16[896,1024]{1,0:T(8,128)(2,1)S(1)}, bf16[896,1024]{1,0:T(8,128)(2,1)}, u32[]{:S(2)}) copy-start(bf16[896,1024]{1,0:T(8,128)(2,1)} %param.14) | copy-start | bytes 5505028
  7.2 6.0 %copy-start.8 = (bf16[8,32,896]{2,1,0:T(8,128)(2,1)S(1)}, bf16[8,32,896]{2,1,0:T(8,128)(2,1)}, u32[]{:S(2)}) copy-start(bf16[8,32,896]{2,1,0:T(8,128)(2,1)} %param.11) | copy-start | bytes 1376260
  7.2 6.2 %copy-start.13 = (f32[896]{0:T(1024)S(1)}, f32[896]{0:T(1024)}, u32[]{:S(2)}) copy-start(f32[896]{0:T(1024)} %param.12) | copy-start | bytes 10756
  13.6 2.3 %copy-start.12 = (bf16[512,256]{1,0:T(8,128)(2,1)S(1)}, bf16[512,256]{1,0:T(8,128)(2,1)}, u32[]{:S(2)}) copy-start(bf16[512,256]{1,0:T(8,128)(2,1)} %mul.124) | copy-start | bytes 786436
  17.3 8.8 %copy-start.9 = (bf16[192,4096]{1,0:T(8,128)(2,1)S(1)}, bf16[192,4096]{1,0:T(8,128)(2,1)}, u32[]{:S(2)}) copy-start(bf16[192,4096]{1,0:T(8,128)(2,1)} %param.9) | copy-start | bytes 4718596
  17.3 31.6 %all-to-all-start = ((bf16[8,64,896]{2,1,0:T(8,128)(2,1)}), bf16[8,64,896]{2,1,0:T(8,128)(2,1)}, u32[]{:S(2)}, u32[]{:S(2)}) async-start(bf16[8,64,896]{2,1,0:T(8,128)(2,1)} %bitcast.2), calls=%async_computation | async-start | bytes 1835008 | tf_op jit(solution)/shard_map/all_to_all | solution.py:148
  24.7 66.5 %all-gather.2.cloned.1.call-start = ((), (), s32[]{:S(2)}) async-start(), calls=%async_computation.1 | async-start | bytes 3440640 | tf_op jit(solution)/shard_map/all_gather | solution.py:156
  27.3 4.7 %collective-permute-start = (bf16[192,1024]{1,0:T(8,128)(2,1)}, bf16[192,1024]{1,0:T(8,128)(2,1)}, u32[]{:S(2)}, u32[]{:S(2)}) collective-permute-start(bf16[192,1024]{1,0:T(8,128)(2,1)} %get-tuple-element.18), channel_id=1, source_target_pairs={{0,1},{1,0},{2,3},{3,2},{4,5},{5,4},{6,7},{7,6},{8,9},{9,8},{10,11... | collective-permute-start | bytes 1179656 | tf_op jit(solution)/shard_map/ppermute | solution.py:96
  27.3 12.2 %collective-permute-start.1 = (bf16[192,1024]{1,0:T(8,128)(2,1)}, bf16[192,1024]{1,0:T(8,128)(2,1)}, u32[]{:S(2)}, u32[]{:S(2)}) collective-permute-start(bf16[192,1024]{1,0:T(8,128)(2,1)} %get-tuple-element.20), channel_id=1, source_target_pairs={{0,2},{1,3},{2,0},{3,1},{4,6},{5,7},{6,4},{7,5},{8,10},{9,11},{10,... | collective-permute-start | bytes 1179656 | tf_op jit(solution)/shard_map/ppermute | solution.py:96
  28.8 18.4 %collective-permute-start.2 = (bf16[192,1024]{1,0:T(8,128)(2,1)}, bf16[192,1024]{1,0:T(8,128)(2,1)}, u32[]{:S(2)}, u32[]{:S(2)}) collective-permute-start(bf16[192,1024]{1,0:T(8,128)(2,1)} %get-tuple-element.17), channel_id=1, source_target_pairs={{0,3},{1,2},{2,1},{3,0},{4,7},{5,6},{6,5},{7,4},{8,11},{9,10},{10,... | collective-permute-start | bytes 1179656 | tf_op jit(solution)/shard_map/ppermute | solution.py:96
  32.0 17.0 %copy-start.11 = (bf16[384,512]{1,0:T(8,128)(2,1)S(1)}, bf16[384,512]{1,0:T(8,128)(2,1)}, u32[]{:S(2)}) copy-start(bf16[384,512]{1,0:T(8,128)(2,1)} %mul.150) | copy-start | bytes 1179652
  54.2 2.2 %collective-permute-start.3 = (bf16[192,1024]{1,0:T(8,128)(2,1)}, bf16[192,1024]{1,0:T(8,128)(2,1)}, u32[]{:S(2)}, u32[]{:S(2)}) collective-permute-start(bf16[192,1024]{1,0:T(8,128)(2,1)} %get-tuple-element.14), channel_id=1, source_target_pairs={{0,1},{1,0},{2,3},{3,2},{4,5},{5,4},{6,7},{7,6},{8,9},{9,8},{10,11... | collective-permute-start | bytes 1179656 | tf_op jit(solution)/shard_map/ppermute | solution.py:96
  54.7 16.2 %collective-permute-start.4 = (bf16[192,1024]{1,0:T(8,128)(2,1)}, bf16[192,1024]{1,0:T(8,128)(2,1)}, u32[]{:S(2)}, u32[]{:S(2)}) collective-permute-start(bf16[192,1024]{1,0:T(8,128)(2,1)} %get-tuple-element.16), channel_id=1, source_target_pairs={{0,2},{1,3},{2,0},{3,1},{4,6},{5,7},{6,4},{7,5},{8,10},{9,11},{10,... | collective-permute-start | bytes 1179656 | tf_op jit(solution)/shard_map/ppermute | solution.py:96
  56.2 30.6 %collective-permute-start.5 = (bf16[192,1024]{1,0:T(8,128)(2,1)}, bf16[192,1024]{1,0:T(8,128)(2,1)}, u32[]{:S(2)}, u32[]{:S(2)}) collective-permute-start(bf16[192,1024]{1,0:T(8,128)(2,1)} %get-tuple-element.13), channel_id=1, source_target_pairs={{0,3},{1,2},{2,1},{3,0},{4,7},{5,6},{6,5},{7,4},{8,11},{9,10},{10,... | collective-permute-start | bytes 1179656 | tf_op jit(solution)/shard_map/ppermute | solution.py:96
  95.9 5.6 %copy-start.3 = (bf16[1536,896]{1,0:T(8,128)(2,1)S(1)}, bf16[1536,896]{1,0:T(8,128)(2,1)}, u32[]{:S(2)}) copy-start(bf16[1536,896]{1,0:T(8,128)(2,1)} %all-gather.2.cloned.1.call-done) | copy-start | bytes 8257540
  95.9 5.6 %copy-start.14 = (bf16[896,1024]{1,0:T(8,128)(2,1)S(1)}, bf16[896,1024]{1,0:T(8,128)(2,1)}, u32[]{:S(2)}) copy-start(bf16[896,1024]{1,0:T(8,128)(2,1)} %param.15) | copy-start | bytes 5505028
  101.5 3.6 %copy-start.2 = (bf16[768,1024]{1,0:T(8,128)(2,1)S(1)}, bf16[768,1024]{1,0:T(8,128)(2,1)}, u32[]{:S(2)}) copy-start(bf16[768,1024]{1,0:T(8,128)(2,1)} %concatenate.9.q_ref) | copy-start | bytes 4718596
  105.2 17.6 %copy-start.4 = (bf16[896,1536]{1,0:T(8,128)(2,1)S(1)}, bf16[896,1536]{1,0:T(8,128)(2,1)}, u32[]{:S(2)}) copy-start(bf16[896,1536]{1,0:T(8,128)(2,1)} %copy.22) | copy-start | bytes 8257540
  125.8 3.2 %copy-start.5 = (f32[2,2,2,112,1024]{4,3,2,1,0:T(8,128)}, f32[2,2,2,112,1024]{4,3,2,1,0:T(8,128)S(1)}, u32[]{:S(2)}) copy-start(f32[2,2,2,112,1024]{4,3,2,1,0:T(8,128)S(1)} %fusion.25) | copy-start | bytes 11010052
  127.0 22.9 %collective-permute-start.12 = (bf16[2,2,112,1024]{3,2,1,0:T(8,128)(2,1)}, bf16[2,2,112,1024]{3,2,1,0:T(8,128)(2,1)}, u32[]{:S(2)}, u32[]{:S(2)}) collective-permute-start(bf16[2,2,112,1024]{3,2,1,0:T(8,128)(2,1)} %fusion.10), channel_id=1, source_target_pairs={{0,4},{4,0},{8,12},{12,8},{16,20},{20,16},{24,28},{28,24},{1,5},{5... | collective-permute-start | bytes 2752520 | tf_op jit(solution)/shard_map/ppermute | solution.py:121
  131.0 9.0 %collective-permute-start.6 = (bf16[192,1024]{1,0:T(8,128)(2,1)S(1)}, bf16[192,1024]{1,0:T(8,128)(2,1)S(1)}, u32[]{:S(2)}, u32[]{:S(2)}) collective-permute-start(bf16[192,1024]{1,0:T(8,128)(2,1)S(1)} %get-tuple-element.22), channel_id=1, source_target_pairs={{0,1},{1,0},{2,3},{3,2},{4,5},{5,4},{6,7},{7,6},{8,9},{9,8},{10,11... | collective-permute-start | bytes 1179656 | tf_op jit(solution)/shard_map/ppermute | solution.py:96
  134.0 2.4 %copy-start.6 = (f32[2,2,2,112,1024]{4,3,2,1,0:T(8,128)}, f32[2,2,2,112,1024]{4,3,2,1,0:T(8,128)S(1)}, u32[]{:S(2)}) copy-start(f32[2,2,2,112,1024]{4,3,2,1,0:T(8,128)S(1)} %fusion.24) | copy-start | bytes 11010052
  134.0 12.3 %collective-permute-start.7 = (bf16[192,1024]{1,0:T(8,128)(2,1)S(1)}, bf16[192,1024]{1,0:T(8,128)(2,1)S(1)}, u32[]{:S(2)}, u32[]{:S(2)}) collective-permute-start(bf16[192,1024]{1,0:T(8,128)(2,1)S(1)} %get-tuple-element.23), channel_id=1, source_target_pairs={{0,2},{1,3},{2,0},{3,1},{4,6},{5,7},{6,4},{7,5},{8,10},{9,11},{10,... | collective-permute-start | bytes 1179656 | tf_op jit(solution)/shard_map/ppermute | solution.py:96
  137.5 23.5 %collective-permute-start.9 = (bf16[2,2,112,1024]{3,2,1,0:T(8,128)(2,1)}, bf16[2,2,112,1024]{3,2,1,0:T(8,128)(2,1)}, u32[]{:S(2)}, u32[]{:S(2)}) collective-permute-start(bf16[2,2,112,1024]{3,2,1,0:T(8,128)(2,1)} %fusion.9), channel_id=1, source_target_pairs={{0,8},{4,12},{8,0},{12,4},{16,24},{20,28},{24,16},{28,20},{1,9},{5... | collective-permute-start | bytes 2752520 | tf_op jit(solution)/shard_map/ppermute | solution.py:121
  138.9 26.1 %collective-permute-start.8 = (bf16[192,1024]{1,0:T(8,128)(2,1)}, bf16[192,1024]{1,0:T(8,128)(2,1)S(1)}, u32[]{:S(2)}, u32[]{:S(2)}) collective-permute-start(bf16[192,1024]{1,0:T(8,128)(2,1)} %get-tuple-element.21), channel_id=1, source_target_pairs={{0,3},{1,2},{2,1},{3,0},{4,7},{5,6},{6,5},{7,4},{8,11},{9,10},{10,... | collective-permute-start | bytes 1179656 | tf_op jit(solution)/shard_map/ppermute | solution.py:96
  149.8 11.2 %copy-start.7 = (f32[2,2,2,112,1024]{4,3,2,1,0:T(8,128)S(1)}, f32[2,2,2,112,1024]{4,3,2,1,0:T(8,128)}, u32[]{:S(2)}) copy-start(f32[2,2,2,112,1024]{4,3,2,1,0:T(8,128)} %copy-done.6) | copy-start | bytes 11010052
  152.2 24.8 %collective-permute-start.13 = (bf16[2,112,1024]{2,1,0:T(8,128)(2,1)S(1)}, bf16[2,112,1024]{2,1,0:T(8,128)(2,1)S(1)}, u32[]{:S(2)}, u32[]{:S(2)}) collective-permute-start(bf16[2,112,1024]{2,1,0:T(8,128)(2,1)S(1)} %fusion.15), channel_id=1, source_target_pairs={{0,8},{4,12},{8,0},{12,4},{16,24},{20,28},{24,16},{28,20},{1,9},{5... | collective-permute-start | bytes 1376264 | tf_op jit(solution)/shard_map/ppermute | solution.py:121
  162.7 28.7 %collective-permute-start.10 = (bf16[2,112,1024]{2,1,0:T(8,128)(2,1)S(1)}, bf16[2,112,1024]{2,1,0:T(8,128)(2,1)S(1)}, u32[]{:S(2)}, u32[]{:S(2)}) collective-permute-start(bf16[2,112,1024]{2,1,0:T(8,128)(2,1)S(1)} %fusion.14), channel_id=1, source_target_pairs={{0,16},{4,20},{8,24},{12,28},{16,0},{20,4},{24,8},{28,12},{1,17},{... | collective-permute-start | bytes 1376264 | tf_op jit(solution)/shard_map/ppermute | solution.py:121
  165.1 26.4 %copy-start.10 = (bf16[192,4096]{1,0:T(8,128)(2,1)}, bf16[192,4096]{1,0:T(8,128)(2,1)S(1)}, u32[]{:S(2)}) copy-start(bf16[192,4096]{1,0:T(8,128)(2,1)S(1)} %constant_dynamic-update-slice_fusion) | copy-start | bytes 4718596
  177.2 16.7 %collective-permute-start.14 = (bf16[112,1024]{1,0:T(8,128)(2,1)S(1)}, bf16[112,1024]{1,0:T(8,128)(2,1)S(1)}, u32[]{:S(2)}, u32[]{:S(2)}) collective-permute-start(bf16[112,1024]{1,0:T(8,128)(2,1)S(1)} %fusion.18), channel_id=1, source_target_pairs={{0,16},{4,20},{8,24},{12,28},{16,0},{20,4},{24,8},{28,12},{1,17},{... | collective-permute-start | bytes 688136 | tf_op jit(solution)/shard_map/ppermute | solution.py:121
  191.4 7.1 %copy-start.1 = (bf16[896,1024]{1,0:T(8,128)(2,1)S(1)}, bf16[896,1024]{1,0:T(8,128)(2,1)}, u32[]{:S(2)}) copy-start(bf16[896,1024]{1,0:T(8,128)(2,1)} %param.14) | copy-start | bytes 5505028
  191.6 6.1 %collective-permute-start.11 = (bf16[112,1024]{1,0:T(8,128)(2,1)S(1)}, bf16[112,1024]{1,0:T(8,128)(2,1)S(1)}, u32[]{:S(2)}, u32[]{:S(2)}) collective-permute-start(bf16[112,1024]{1,0:T(8,128)(2,1)S(1)} %fusion.17), channel_id=1, source_target_pairs={{0,4},{4,0},{8,12},{12,8},{16,20},{20,16},{24,28},{28,24},{1,5},{5... | collective-permute-start | bytes 688136 | tf_op jit(solution)/shard_map/ppermute | solution.py:121
Sparse Core Ops, SparseCore 0:
  51.7 38.9 all-gather.1
